TPU v7x, 32 devices: a whole 2x2x4 slice. The times are simulated.
32 devices in a mesh: dp: 8 (over z, y), mp: 4 (over x, core).
Axes of the slice: x: 2, y: 2, z: 4, core: 2. Of those that a mesh axis runs over, the one named last changes fastest.
Arguments:
- tokens: bfloat16 [10240, 1024], P(('dp', 'mp')), may hold values from -6 to 6
- cotangent: bfloat16 [10240, 1024], P(('dp', 'mp')), may hold values from -6 to 6
- in_gain: float32 [2, 1024], replicated, may hold values from 0.1 to 1.9
- w_z: bfloat16 [2, 1024, 2048], P(None, 'dp', 'mp'), may hold values from -0.1875 to 0.1875
- w_x: bfloat16 [2, 1024, 2048], P(None, 'dp', 'mp'), may hold values from -0.1875 to 0.1875
- w_bc: bfloat16 [2, 1024, 256], P(None, 'dp'), may hold values from -0.1875 to 0.1875
- w_dt: bfloat16 [2, 1024, 32], P(None, 'dp', 'mp'), may hold values from -0.1875 to 0.1875
- conv_x_w: float32 [2, 4, 2048], P(None, None, 'mp'), may hold values from -3 to 3
- conv_x_b: float32 [2, 2048], P(None, 'mp'), may hold values from -3 to 3
- conv_bc_w: float32 [2, 4, 256], replicated, may hold values from -3 to 3
- conv_bc_b: float32 [2, 256], replicated, may hold values from -3 to 3
- dt_bias: float32 [2, 32], P(None, 'mp'), may hold values from -6.9 to -2.25
- a_log: float32 [2, 32], P(None, 'mp'), may hold values from 0 to 2.77
- dskip: float32 [2, 32], P(None, 'mp'), may hold values from 0.5 to 1.5
- norm_gain: float32 [2, 2048], P(None, 'mp'), may hold values from 0.1 to 1.9
- w_out: bfloat16 [2, 2048, 1024], P(None, 'mp', 'dp'), may hold values from -0.125 to 0.125
Outputs:
- outputs: float32 [10240, 1024], P(('dp', 'mp'))
- d_tokens: float32 [10240, 1024], P(('dp', 'mp'))
- g_in_gain: float32 [2, 1024], replicated
- g_w_z: float32 [2, 1024, 2048], P(None, 'dp', 'mp')
- g_w_x: float32 [2, 1024, 2048], P(None, 'dp', 'mp')
- g_w_bc: float32 [2, 1024, 256], P(None, 'dp')
- g_w_dt: float32 [2, 1024, 32], P(None, 'dp', 'mp')
- g_conv_x_w: float32 [2, 4, 2048], P(None, None, 'mp')
- g_conv_x_b: float32 [2, 2048], P(None, 'mp')
- g_conv_bc_w: float32 [2, 4, 256], replicated
- g_conv_bc_b: float32 [2, 256], replicated
- g_dt_bias: float32 [2, 32], P(None, 'mp')
- g_a_log: float32 [2, 32], P(None, 'mp')
- g_dskip: float32 [2, 32], P(None, 'mp')
- g_norm_gain: float32 [2, 2048], P(None, 'mp')
- g_w_out: float32 [2, 2048, 1024], P(None, 'mp', 'dp')
All inputs are finite; a program needn't handle non-finite values.
Results may differ from a plain program's by a relative error of at most 0.0098.
Values may be sent and summed in bfloat16 or wider, within the bound.
A program may use at most 192 MiB of HBM per device.

v0:
```python
import jax
import jax.numpy as jnp
from jax import lax
from jax.sharding import PartitionSpec as P

INNER = 2048
HEADDIM = 64
STATE = 128
SPAN = 256
LEN = 1280


epsilon = 1e-05
HIGHEST_PRECISION = lax.Precision.HIGHEST


def causal_conv(values, kernel, offset, seq_len):
    rows, width = values.shape
    taps = kernel.shape[0]
    seqs = values.reshape(rows // seq_len, seq_len, width)
    padded = jnp.pad(seqs, ((0, 0), (taps - 1, 0), (0, 0)))
    summed = offset + jnp.zeros_like(seqs)
    for shift_tap in range(taps):
        summed = summed + padded[:, shift_tap : shift_tap + seq_len, :] * kernel[shift_tap]
    return jax.nn.silu(summed).reshape(rows, width)


def span_step(rate, state, block):
    inputs, steps, keys, reads = block
    logs = jnp.cumsum(steps * rate, axis=1)
    heads_first = jnp.swapaxes(logs, 1, 2)
    differ = heads_first[:, :, :, None] - heads_first[:, :, None, :]
    length = logs.shape[1]
    lower = jnp.arange(length)[:, None] >= jnp.arange(length)[None, :]
    decays = jnp.exp(jnp.where(lower, differ, -1e30))
    scores = jnp.einsum("sin,sjn->sij", reads, keys, precision=HIGHEST_PRECISION)
    weights = scores[:, None] * decays * jnp.swapaxes(steps, 1, 2)[:, :, None, :]
    inner_out = jnp.einsum("shij,sjhp->sihp", weights, inputs, precision=HIGHEST_PRECISION)
    carried = (
        jnp.einsum("sin,shnp->sihp", reads, state, precision=HIGHEST_PRECISION)
        * jnp.exp(logs)[..., None]
    )
    last_log = logs[:, -1, :]
    tails = jnp.exp(last_log[:, None, :] - logs) * steps
    update = jnp.einsum(
        "sjn,sjhp->shnp", keys, inputs * tails[..., None], precision=HIGHEST_PRECISION
    )
    new_state = state * jnp.exp(last_log)[:, :, None, None] + update
    return (new_state, inner_out + carried)


def state_scan(inputs, steps, rate, keys, reads):
    rows = inputs.shape[0]
    heads = steps.shape[1]
    seqs = rows // LEN
    count = LEN // SPAN

    def split_blocks(value):
        value = value.reshape((seqs, count, SPAN) + value.shape[1:])
        return jnp.moveaxis(value, 1, 0)

    blocks = (
        split_blocks(inputs.reshape(rows, heads, HEADDIM)),
        split_blocks(steps),
        split_blocks(keys),
        split_blocks(reads),
    )
    start_state = jnp.zeros((seqs, heads, STATE, HEADDIM), jnp.float32)
    step_fn = jax.checkpoint(lambda state, block: span_step(rate, state, block))
    final_state, outs = lax.scan(step_fn, start_state, blocks)
    return jnp.moveaxis(outs, 0, 1).reshape(rows, heads * HEADDIM)


def mixer_part(x_raw, bc_act, dt_raw, conv_w, conv_b, dt_off, log_rate, skip_coef):
    x_act = causal_conv(x_raw, conv_w, conv_b, LEN)
    steps = jax.nn.softplus(dt_raw + dt_off)
    scanned = state_scan(x_act, steps, -jnp.exp(log_rate), bc_act[:, :STATE], bc_act[:, STATE:])
    return scanned + x_act * jnp.repeat(skip_coef, HEADDIM)


def bc_conv(bc_raw, kernel, offset):
    return causal_conv(bc_raw, kernel, offset, LEN)


def project_back(values, weight):
    return lax.dot_general(
        values, weight, (((1,), (1,)), ((), ())), preferred_element_type=jnp.float32
    )


def over_rows(left, right):
    return lax.dot_general(
        left, right, (((0,), (0,)), ((), ())), preferred_element_type=jnp.float32
    )


def body(
    tokens,
    cotangent,
    in_gain,
    w_z,
    w_x,
    w_bc,
    w_dt,
    conv_x_w,
    conv_x_b,
    conv_bc_w,
    conv_bc_b,
    dt_bias,
    a_log,
    dskip,
    norm_gain,
    w_out,
):
    layers = w_z.shape[0]
    own_rows = tokens.shape[0]
    current = tokens.astype(jnp.float32)
    saved = []
    for depth in range(layers):
        weights = (
            lax.all_gather(w_z[depth], "dp", axis=0, tiled=True),
            lax.all_gather(w_x[depth], "dp", axis=0, tiled=True),
            lax.all_gather(w_bc[depth], "dp", axis=0, tiled=True),
            lax.all_gather(w_dt[depth], "dp", axis=0, tiled=True),
            lax.all_gather(w_out[depth], "dp", axis=1, tiled=True),
        )
        scale = lax.rsqrt(jnp.mean(current * current, axis=-1, keepdims=True) + epsilon)
        normed = (current * scale * in_gain[depth]).astype(jnp.bfloat16)
        gathered = lax.all_gather(normed, "mp", axis=0, tiled=True)
        z_val = jnp.dot(gathered, weights[0], preferred_element_type=jnp.float32)
        x_raw = jnp.dot(gathered, weights[1], preferred_element_type=jnp.float32)
        bc_raw = jnp.dot(gathered, weights[2], preferred_element_type=jnp.float32)
        dt_raw = jnp.dot(gathered, weights[3], preferred_element_type=jnp.float32)
        bc_act = bc_conv(bc_raw, conv_bc_w[depth], conv_bc_b[depth])
        mixed_y = mixer_part(
            x_raw,
            bc_act,
            dt_raw,
            conv_x_w[depth],
            conv_x_b[depth],
            dt_bias[depth],
            a_log[depth],
            dskip[depth],
        )
        gated = mixed_y * jax.nn.silu(z_val)
        squares = lax.psum(jnp.sum(gated * gated, axis=-1), "mp")
        ratio = lax.rsqrt(squares / INNER + epsilon)[:, None]
        mixed = (gated * ratio * norm_gain[depth]).astype(jnp.bfloat16)
        w_down = weights[4]
        branch = lax.psum_scatter(
            jnp.dot(mixed, w_down, preferred_element_type=jnp.float32),
            "mp",
            scatter_dimension=0,
            tiled=True,
        )
        held = None
        saved.append((current, scale, normed, z_val, x_raw, bc_raw, dt_raw, ratio, held))
        current = current + branch
    result = current
    gradient = cotangent.astype(jnp.float32)
    offset = lax.axis_index("mp") * own_rows
    list_in_gain, list_proj, list_small = ([], [], [])
    for depth in reversed(range(layers)):
        current, scale, normed, z_val, x_raw, bc_raw, dt_raw, ratio, held = saved[depth]
        weights = (
            lax.all_gather(w_z[depth], "dp", axis=0, tiled=True),
            lax.all_gather(w_x[depth], "dp", axis=0, tiled=True),
            lax.all_gather(w_bc[depth], "dp", axis=0, tiled=True),
            lax.all_gather(w_dt[depth], "dp", axis=0, tiled=True),
            lax.all_gather(w_out[depth], "dp", axis=1, tiled=True),
        )
        gathered = lax.all_gather(normed, "mp", axis=0, tiled=True)
        w_gate, w_inner, w_pair, w_step, w_down = weights
        grad_rows = lax.all_gather(gradient.astype(jnp.bfloat16), "mp", axis=0, tiled=True)
        bc_act, bc_pull = jax.vjp(bc_conv, bc_raw, conv_bc_w[depth], conv_bc_b[depth])
        mixed_y, mix_pull = jax.vjp(
            mixer_part,
            x_raw,
            bc_act,
            dt_raw,
            conv_x_w[depth],
            conv_x_b[depth],
            dt_bias[depth],
            a_log[depth],
            dskip[depth],
        )
        gate_act = jax.nn.silu(z_val)
        gated = mixed_y * gate_act
        normal = gated * ratio
        mixed = (normal * norm_gain[depth]).astype(jnp.bfloat16)
        g_down = over_rows(mixed, grad_rows)
        d_mixed = project_back(grad_rows, w_down)
        g_gain_norm = jnp.sum(d_mixed * normal, axis=0)
        weighted = d_mixed * norm_gain[depth]
        products = lax.psum(jnp.sum(weighted * gated, axis=-1), "mp")
        d_gated = ratio * weighted - gated * ratio * ratio * ratio * (products / INNER)[:, None]
        sigmoid_z = jax.nn.sigmoid(z_val)
        d_y = d_gated * gate_act
        d_z = d_gated * mixed_y * sigmoid_z * (1.0 + z_val * (1.0 - sigmoid_z))
        d_xr, d_bc_part, d_dtr, g_cxw, g_cxb, g_dtb, g_alog, g_skip = mix_pull(d_y)
        d_bc_act = lax.psum(d_bc_part, "mp")
        d_bcr, g_cbw, g_cbb = bc_pull(d_bc_act)
        z_low = d_z.astype(jnp.bfloat16)
        x_low = d_xr.astype(jnp.bfloat16)
        bc_low = d_bcr.astype(jnp.bfloat16)
        dt_low = d_dtr.astype(jnp.bfloat16)
        summed = project_back(z_low, w_gate) + project_back(x_low, w_inner)
        d_normed = lax.psum_scatter(
            summed + project_back(dt_low, w_step), "mp", scatter_dimension=0, tiled=True
        )
        d_normed = d_normed + project_back(
            lax.dynamic_slice_in_dim(bc_low, offset, own_rows, 0), w_pair
        )
        proj_grads = (
            lax.psum_scatter(over_rows(gathered, z_low), "dp", scatter_dimension=0, tiled=True),
            lax.psum_scatter(over_rows(gathered, x_low), "dp", scatter_dimension=0, tiled=True),
            lax.psum_scatter(over_rows(gathered, bc_low), "dp", scatter_dimension=0, tiled=True),
            lax.psum_scatter(over_rows(gathered, dt_low), "dp", scatter_dimension=0, tiled=True),
            lax.psum_scatter(g_down, "dp", scatter_dimension=1, tiled=True),
        )
        gained = d_normed * in_gain[depth]
        list_in_gain.append(jnp.sum(d_normed * current * scale, axis=0))
        gradient = (
            gradient
            + scale * gained
            - current * scale * scale * scale * jnp.mean(gained * current, axis=-1, keepdims=True)
        )
        list_proj.append(proj_grads)
        list_small.append((g_cxw, g_cxb, g_cbw, g_cbb, g_dtb, g_alog, g_skip, g_gain_norm))
    list_in_gain = list_in_gain[::-1]
    list_proj = list_proj[::-1]
    list_small = list_small[::-1]
    stacked_proj = [jnp.stack([entry[member] for entry in list_proj]) for member in range(5)]
    stacked_small = [jnp.stack([entry[member] for entry in list_small]) for member in range(8)]
    small_sums = lax.psum(
        (
            stacked_small[0],
            stacked_small[1],
            stacked_small[2],
            stacked_small[3],
            stacked_small[4],
            stacked_small[5],
            stacked_small[6],
            stacked_small[7],
        ),
        "dp",
    )
    gain_sums = lax.psum(jnp.stack(list_in_gain), ("dp", "mp"))
    return (
        result,
        gradient,
        gain_sums,
        stacked_proj[0],
        stacked_proj[1],
        stacked_proj[2],
        stacked_proj[3],
        small_sums[0],
        small_sums[1],
        small_sums[2],
        small_sums[3],
        small_sums[4],
        small_sums[5],
        small_sums[6],
        small_sums[7],
        stacked_proj[4],
    )


def solution(mesh):
    placed = (
        P(("dp", "mp"), None),
        P(("dp", "mp"), None),
        P(),
        P(None, "dp", "mp"),
        P(None, "dp", "mp"),
        P(None, "dp", None),
        P(None, "dp", "mp"),
        P(None, None, "mp"),
        P(None, "mp"),
        P(),
        P(),
        P(None, "mp"),
        P(None, "mp"),
        P(None, "mp"),
        P(None, "mp"),
        P(None, "mp", "dp"),
    )
    return jax.shard_map(
        body,
        mesh=mesh,
        in_specs=placed,
        out_specs=(
            P(("dp", "mp"), None),
            P(("dp", "mp"), None),
            P(),
            P(None, "dp", "mp"),
            P(None, "dp", "mp"),
            P(None, "dp", None),
            P(None, "dp", "mp"),
            P(None, None, "mp"),
            P(None, "mp"),
            P(),
            P(),
            P(None, "mp"),
            P(None, "mp"),
            P(None, "mp"),
            P(None, "mp"),
            P(None, "mp", "dp"),
        ),
        check_vma=False,
    )
```

profile of v0, /device:TPU:0, one launch (start us, length us, event | category | flops | bytes accessed | tf_op | source)
XLA Modules:
  0.0 1846.5 jit_solution(12051371190748344395)
XLA Ops:
  14.2 33.1 %all-gather.2 = bf16[1,1024,256]{2,1,0:T(8,128)(2,1)S(1)} all-gather(bf16[1,128,256]{2,1,0:T(8,128)(2,1)S(1)} %get-tuple-element.1623), channel_id=4, replica_groups=mesh['dp'=8,'mp'=4] {'dp'}, dimensions={1}, use_global_device_ids=true | all-gather | bytes 589824 | tf_op jit(solution)/shard_map/all_gather | solution.py:123
  47.6 26.2 %all-gather = bf16[1,1024,8]{1,2,0:T(8,128)(2,1)S(1)} all-gather(bf16[1,128,8]{1,2,0:T(8,128)(2,1)S(1)} %get-tuple-element.1647), channel_id=2, replica_groups=mesh['dp'=8,'mp'=4] {'dp'}, dimensions={1}, use_global_device_ids=true | all-gather | bytes 18432 | tf_op jit(solution)/shard_map/all_gather | solution.py:124
  95.0 5.4 copy.216
  105.3 52.2 %while.108 = (s32[]{:T(128)}, f32[1,8,128,64]{2,3,1,0:T(8,128)S(1)}, f32[5,1,256,8,64]{2,4,3,1,0:T(8,128)}, f32[5,1,256,8]{2,3,1,0:T(8,128)}, f32[8]{0:T(128)}, ...) while((s32[]{:T(128)}, f32[1,8,128,64]{2,3,1,0:T(8,128)S(1)}, ...), condition=%wide.region_4.5_spmd.clone, body=%wide.region_1.4_spmd.clone.sunk | while | flops 908992512 | bytes 5271919 | solution.py:70
  157.5 5.4 copy.262
  168.0 7.6 multiply_reduce_fusion.23
  175.6 5.7 psum.105
  181.4 5.1 fusion.358
  187.0 50.1 %reduce-scatter.15.cloned.1.call-done = f32[320,1024]{1,0:T(8,128)} async-done(((f32[1280,1024]{1,0:T(8,128)}), f32[320,1024]{1,0:T(8,128)}) %reduce-scatter.15.cloned.1.call-update) | async-done | bytes 1310736 | tf_op jit(solution)/shard_map/reduce_scatter | solution.py:150
  244.2 31.5 %all-gather.7 = bf16[1,1024,256]{2,1,0:T(8,128)(2,1)S(1)} all-gather(bf16[1,128,256]{2,1,0:T(8,128)(2,1)S(1)} %get-tuple-element.1622), channel_id=9, replica_groups=mesh['dp'=8,'mp'=4] {'dp'}, dimensions={1}, use_global_device_ids=true | all-gather | bytes 589824 | tf_op jit(solution)/shard_map/all_gather | solution.py:123
  275.7 26.2 %all-gather.5 = bf16[1,1024,8]{1,2,0:T(8,128)(2,1)S(1)} all-gather(bf16[1,128,8]{1,2,0:T(8,128)(2,1)S(1)} %get-tuple-element.1646), channel_id=7, replica_groups=mesh['dp'=8,'mp'=4] {'dp'}, dimensions={1}, use_global_device_ids=true | all-gather | bytes 18432 | tf_op jit(solution)/shard_map/all_gather | solution.py:124
  321.5 5.4 copy.223
  331.9 52.2 %while.109 = (s32[]{:T(128)}, f32[1,8,128,64]{2,3,1,0:T(8,128)S(1)}, f32[5,1,256,8,64]{2,4,3,1,0:T(8,128)}, f32[5,1,256,8]{2,3,1,0:T(8,128)}, f32[8]{0:T(128)}, ...) while((s32[]{:T(128)}, f32[1,8,128,64]{2,3,1,0:T(8,128)S(1)}, ...), condition=%wide.region_12.13_spmd.clone, body=%wide.region_9.12_spmd.clone.sunk | while | flops 908992512 | bytes 5271919 | solution.py:70
  387.2 55.4 %while.110 = (s32[]{:T(128)}, f32[1,8,128,64]{2,3,1,0:T(8,128)S(1)}, f32[5,1,256,8,64]{2,4,3,1,0:T(8,128)}, f32[5,1,8,128,64]{3,4,2,1,0:T(8,128)}, f32[5,1,256,8...) while((s32[]{:T(128)}, f32[1,8,128,64]{2,3,1,0:T(8,128)S(1)}, ...), condition=%wide.region_19.21_spmd.clone, body=%wide.region_16.20_spmd.clone.sunk | while | flops 908926976 | bytes 5469055 | solution.py:70
  462.6 8.5 multiply_reduce_fusion.22
  471.1 5.7 psum.106
  476.9 10.3 multiply_reduce_fusion.10
  487.2 6.6 psum.107
  493.9 7.9 fusion.336
  506.7 5.3 copy.240
  516.2 148.3 %while.111 = (s32[]{:T(128)}, f32[8]{0:T(128)}, f32[1,8,128,64]{2,3,1,0:T(8,128)S(1)}, f32[5,1,256,8,64]{2,4,3,1,0:T(8,128)}, f32[5,1,256,8]{2,3,1,0:T(8,128)}, ...) while((s32[]{:T(128)}, f32[8]{0:T(128)}, ...), condition=%wide.region_36.38_spmd.clone, body=%wide.region_22.37_spmd.clone.sunk | while | flops 2124980224 | bytes 20590004 | solution.py:70
  671.4 5.2 reshape.2302
  676.6 5.1 multiply_reduce_fusion.14
  693.2 11.4 all-reduce.46.cloned.1.call-done
  709.3 49.3 %reduce-scatter.19.cloned.1.call-done = f32[320,1024]{1,0:T(8,128)} async-done(((f32[1280,1024]{1,0:T(8,128)}), f32[320,1024]{1,0:T(8,128)}) %reduce-scatter.19.cloned.1.call-update) | async-done | bytes 1310736 | tf_op jit(solution)/shard_map/reduce_scatter | solution.py:208
  766.9 55.6 %while.112 = (s32[]{:T(128)}, f32[1,8,128,64]{2,3,1,0:T(8,128)S(1)}, f32[5,1,256,8,64]{2,4,3,1,0:T(8,128)}, f32[5,1,8,128,64]{3,4,2,1,0:T(8,128)}, f32[5,1,256,8...) while((s32[]{:T(128)}, f32[1,8,128,64]{2,3,1,0:T(8,128)S(1)}, ...), condition=%wide.region_43.45_spmd.clone, body=%wide.region_40.44_spmd.clone.sunk | while | flops 908926976 | bytes 5469055 | solution.py:70
  832.7 8.5 multiply_reduce_fusion.11
  841.1 5.8 psum.109
  847.0 7.9 fusion.337
  859.8 5.3 copy.256
  869.2 148.0 %while.113 = (s32[]{:T(128)}, f32[8]{0:T(128)}, f32[1,8,128,64]{2,3,1,0:T(8,128)S(1)}, f32[5,1,256,8,64]{2,4,3,1,0:T(8,128)}, f32[5,1,256,8]{2,3,1,0:T(8,128)}, ...) while((s32[]{:T(128)}, f32[8]{0:T(128)}, ...), condition=%wide.region_60.62_spmd.clone, body=%wide.region_46.61_spmd.clone.sunk | while | flops 2124980224 | bytes 20590004 | solution.py:70
  1028.4 31.5 %all-reduce.48.cloned.1.call-done = f32[1,1280,256]{2,1,0:T(8,128)} async-done(((f32[1,1280,256]{2,1,0:T(8,128)}), f32[1,1280,256]{2,1,0:T(8,128)}) %all-reduce.48.cloned.1.call-update) | async-done | bytes 1310736 | tf_op jit(solution)/shard_map/psum | solution.py:201
  1071.5 5.7 fusion.360
  1086.6 5.2 reshape.2305
  1122.8 5.1 fusion.359
  1129.3 43.8 %reduce-scatter.35.cloned.1.call-done = f32[128,8]{0,1:T(8,128)} async-done(((f32[1024,8]{0,1:T(8,128)}), f32[128,8]{0,1:T(8,128)}) %reduce-scatter.35.cloned.1.call-update) | async-done | bytes 4112 | tf_op jit(solution)/shard_map/reduce_scatter | solution.py:218
  1174.5 36.7 %all-reduce.42 = (f32[2,4,512]{2,1,0:T(4,128)}, f32[2,512]{1,0:T(2,128)}, f32[2,4,256]{2,1,0:T(4,128)}, f32[2,256]{1,0:T(2,128)}, f32[2,8]{1,0:T(2,128)}, /*inde...) all-reduce(f32[2,4,512]{2,1,0:T(4,128)S(1)} %pad_maximum_fusion.4, ...), channel_id=1, replica_groups=mesh['dp'=8,'mp'=4] {'dp'}, use_global_device_ids=true, to_apply=%region_83.85 | all-reduce | flops 8752 | bytes 70016 | tf_op jit(solution)/shard_map/psum | solution.py:235
  1211.2 27.7 %reduce-scatter.33.cloned.1.call-done = f32[128,256]{1,0:T(8,128)} async-done(((f32[1024,256]{1,0:T(8,128)}), f32[128,256]{1,0:T(8,128)}) %reduce-scatter.33.cloned.1.call-update) | async-done | bytes 131088 | tf_op jit(solution)/shard_map/reduce_scatter | solution.py:217
  1238.9 66.7 %reduce-scatter.31.cloned.1.call-done = f32[128,256]{1,0:T(8,128)} async-done(((f32[1024,256]{1,0:T(8,128)}), f32[128,256]{1,0:T(8,128)}) %reduce-scatter.31.cloned.1.call-update) | async-done | bytes 131088 | tf_op jit(solution)/shard_map/reduce_scatter | solution.py:217
  1307.4 69.1 %reduce-scatter.41.cloned.1.call-done = f32[512,128]{1,0:T(8,128)} async-done(((f32[512,1024]{1,0:T(8,128)}), f32[512,128]{1,0:T(8,128)}) %reduce-scatter.41.cloned.1.call-update) | async-done | bytes 262160 | tf_op jit(solution)/shard_map/reduce_scatter | solution.py:219
  1376.4 70.8 %reduce-scatter.39.cloned.1.call-done = f32[512,128]{1,0:T(8,128)} async-done(((f32[512,1024]{1,0:T(8,128)}), f32[512,128]{1,0:T(8,128)}) %reduce-scatter.39.cloned.1.call-update) | async-done | bytes 262160 | tf_op jit(solution)/shard_map/reduce_scatter | solution.py:219
  1449.1 68.4 %reduce-scatter.29.cloned.1.call-done = f32[128,512]{1,0:T(8,128)} async-done(((f32[1024,512]{1,0:T(8,128)}), f32[128,512]{1,0:T(8,128)}) %reduce-scatter.29.cloned.1.call-update) | async-done | bytes 262160 | tf_op jit(solution)/shard_map/reduce_scatter | solution.py:216
  1517.5 70.1 %reduce-scatter.27.cloned.1.call-done = f32[128,512]{1,0:T(8,128)} async-done(((f32[1024,512]{1,0:T(8,128)}), f32[128,512]{1,0:T(8,128)}) %reduce-scatter.27.cloned.1.call-update) | async-done | bytes 262160 | tf_op jit(solution)/shard_map/reduce_scatter | solution.py:216
  1589.5 68.4 %reduce-scatter.25.cloned.1.call-done = f32[128,512]{1,0:T(8,128)} async-done(((f32[1024,512]{1,0:T(8,128)}), f32[128,512]{1,0:T(8,128)}) %reduce-scatter.25.cloned.1.call-update) | async-done | bytes 262160 | tf_op jit(solution)/shard_map/reduce_scatter | solution.py:215
  1657.8 69.9 %reduce-scatter.23.cloned.1.call-done = f32[128,512]{1,0:T(8,128)} async-done(((f32[1024,512]{1,0:T(8,128)}), f32[128,512]{1,0:T(8,128)}) %reduce-scatter.23.cloned.1.call-update) | async-done | bytes 262160 | tf_op jit(solution)/shard_map/reduce_scatter | solution.py:215
  1729.6 51.2 %reduce-scatter.21.cloned.1.call-done = f32[320,1024]{1,0:T(8,128)} async-done(((f32[1280,1024]{1,0:T(8,128)}), f32[320,1024]{1,0:T(8,128)}) %reduce-scatter.21.cloned.1.call-update) | async-done | bytes 1310736 | tf_op jit(solution)/shard_map/reduce_scatter | solution.py:208
  1784.0 39.7 %psum.111 = f32[2,1024]{1,0:T(2,128)} all-reduce(f32[2,1024]{1,0:T(2,128)S(1)} %pad_maximum_fusion.5), channel_id=1, replica_groups=mesh['dp'=8,'mp'=4] {'dp','mp'}, use_global_device_ids=true, to_apply=%region_66.68 | all-reduce | flops 2048 | bytes 16384 | tf_op jit(solution)/shard_map/psum | solution.py:248
  1823.7 11.8 reduce-scatter.17.cloned.1.call-done
  (1505 shorter events, 740.3 us)
Async XLA Ops:
  7.2 67.3 %all-gather.21.cloned.1.call-start = ((), (), s32[]{:S(2)}) async-start(), calls=%async_computation.14 | async-start | bytes 3276800 | tf_op jit(solution)/shard_map/all_gather | solution.py:129
  8.1 230.7 %copy-start.86 = (f32[1,1024]{1,0:T(1,128)}, f32[1,1024]{1,0:T(1,128)S(1)}, u32[]{:S(2)}) copy-start(f32[1,1024]{1,0:T(1,128)S(1)} %get-tuple-element.1640) | copy-start | bytes 12292
  11.7 71.4 %all-gather.29.cloned.1.call-start = ((), (), s32[]{:S(2)}) async-start(), calls=%async_computation.34 | async-start | bytes 1179648 | tf_op jit(solution)/shard_map/all_gather | solution.py:122
  12.5 155.5 %all-gather.31.cloned.1.call-start = ((), (), s32[]{:S(2)}) async-start(), calls=%async_computation.35 | async-start | bytes 1179648 | tf_op jit(solution)/shard_map/all_gather | solution.py:121
  13.3 168.1 %all-gather.33.cloned.1.call-start = ((), (), s32[]{:S(2)}) async-start(), calls=%async_computation.36 | async-start | bytes 1179648 | tf_op jit(solution)/shard_map/all_gather | solution.py:125
  14.1 223.0 %reduce-scatter.15.cloned.1.call-start = ((), (), s32[]{:S(2)}) async-start(), calls=%async_computation.15 | async-start | bytes 6553600 | tf_op jit(solution)/shard_map/reduce_scatter | solution.py:150
  47.4 257.4 %copy-start.140 = (f32[1,1,256]{2,1,0:T(1,128)}, f32[1,1,256]{2,1,0:T(1,128)S(1)}, u32[]{:S(2)}) copy-start(f32[1,1,256]{2,1,0:T(1,128)S(1)} %get-tuple-element.1632) | copy-start | bytes 3076
  47.4 257.4 %copy-start.142 = (f32[1,1,256]{2,1,0:T(1,128)}, f32[1,1,256]{2,1,0:T(1,128)S(1)}, u32[]{:S(2)}) copy-start(f32[1,1,256]{2,1,0:T(1,128)S(1)} %get-tuple-element.1633) | copy-start | bytes 3076
  47.4 257.4 %copy-start.144 = (f32[1,1,256]{2,1,0:T(1,128)}, f32[1,1,256]{2,1,0:T(1,128)S(1)}, u32[]{:S(2)}) copy-start(f32[1,1,256]{2,1,0:T(1,128)S(1)} %get-tuple-element.1638) | copy-start | bytes 3076
  47.4 257.4 %copy-start.146 = (f32[1,1,256]{2,1,0:T(1,128)}, f32[1,1,256]{2,1,0:T(1,128)S(1)}, u32[]{:S(2)}) copy-start(f32[1,1,256]{2,1,0:T(1,128)S(1)} %get-tuple-element.1639) | copy-start | bytes 3076
  47.5 265.7 %copy-start.120 = (f32[1,1,512]{2,1,0:T(1,128)}, f32[1,1,512]{2,1,0:T(1,128)S(1)}, u32[]{:S(2)}) copy-start(f32[1,1,512]{2,1,0:T(1,128)S(1)} %get-tuple-element.1624) | copy-start | bytes 6148
  47.5 265.7 %copy-start.122 = (f32[1,1,512]{2,1,0:T(1,128)}, f32[1,1,512]{2,1,0:T(1,128)S(1)}, u32[]{:S(2)}) copy-start(f32[1,1,512]{2,1,0:T(1,128)S(1)} %get-tuple-element.1625) | copy-start | bytes 6148
  47.5 265.7 %copy-start.124 = (f32[1,1,512]{2,1,0:T(1,128)}, f32[1,1,512]{2,1,0:T(1,128)S(1)}, u32[]{:S(2)}) copy-start(f32[1,1,512]{2,1,0:T(1,128)S(1)} %get-tuple-element.1630) | copy-start | bytes 6148
  47.5 265.7 %copy-start.126 = (f32[1,1,512]{2,1,0:T(1,128)}, f32[1,1,512]{2,1,0:T(1,128)S(1)}, u32[]{:S(2)}) copy-start(f32[1,1,512]{2,1,0:T(1,128)S(1)} %get-tuple-element.1631) | copy-start | bytes 6148
  74.5 93.5 %copy-start.98 = (f32[512]{0:T(512)}, f32[512]{0:T(512)S(1)}, u32[]{:S(2)}) copy-start(f32[512]{0:T(512)S(1)} %mul.1843) | copy-start | bytes 6148
  74.5 106.9 %copy-start.83 = (f32[1,512]{1,0:T(1,128)}, f32[1,512]{1,0:T(1,128)S(1)}, u32[]{:S(2)}) copy-start(f32[1,512]{1,0:T(1,128)S(1)} %get-tuple-element.1643) | copy-start | bytes 6148
  74.5 419.3 %copy-start.81 = (f32[1,512]{1,0:T(1,128)}, f32[1,512]{1,0:T(1,128)S(1)}, u32[]{:S(2)}) copy-start(f32[1,512]{1,0:T(1,128)S(1)} %get-tuple-element.1642) | copy-start | bytes 6148
  186.6 115.5 %all-gather.23.cloned.1.call-start = ((), (), s32[]{:S(2)}) async-start(), calls=%async_computation.16 | async-start | bytes 3276800 | tf_op jit(solution)/shard_map/all_gather | solution.py:129
  240.8 68.9 %all-gather.35.cloned.1.call-start = ((), (), s32[]{:S(2)}) async-start(), calls=%async_computation.37 | async-start | bytes 1179648 | tf_op jit(solution)/shard_map/all_gather | solution.py:122
  241.5 221.0 %all-gather.37.cloned.1.call-start = ((), (), s32[]{:S(2)}) async-start(), calls=%async_computation.38 | async-start | bytes 1179648 | tf_op jit(solution)/shard_map/all_gather | solution.py:121
  242.3 234.6 %all-gather.39.cloned.1.call-start = ((), (), s32[]{:S(2)}) async-start(), calls=%async_computation.39 | async-start | bytes 1179648 | tf_op jit(solution)/shard_map/all_gather | solution.py:125
  243.0 233.9 %all-gather.25.cloned.1.call-start = ((), (), s32[]{:S(2)}) async-start(), calls=%async_computation.18 | async-start | bytes 3276800 | tf_op jit(solution)/shard_map/all_gather | solution.py:174
  243.6 461.0 %all-reduce.46.cloned.1.call-start = ((), (), s32[]{:S(2)}) async-start(), calls=%async_computation.20 | async-start | bytes 2621440 | tf_op jit(solution)/shard_map/psum | solution.py:201
  302.1 191.8 %copy-start.101 = (f32[512]{0:T(512)}, f32[512]{0:T(512)S(1)}, u32[]{:S(2)}) copy-start(f32[512]{0:T(512)S(1)} %mul.1888) | copy-start | bytes 6148
  667.1 91.5 %reduce-scatter.19.cloned.1.call-start = ((), (), s32[]{:S(2)}) async-start(), calls=%async_computation.19 | async-start | bytes 6553600 | tf_op jit(solution)/shard_map/reduce_scatter | solution.py:208
  693.1 139.5 %all-gather.27.cloned.1.call-start = ((), (), s32[]{:S(2)}) async-start(), calls=%async_computation.21 | async-start | bytes 3276800 | tf_op jit(solution)/shard_map/all_gather | solution.py:174
  763.8 296.1 %all-reduce.48.cloned.1.call-start = ((), (), s32[]{:S(2)}) async-start(), calls=%async_computation.23 | async-start | bytes 2621440 | tf_op jit(solution)/shard_map/psum | solution.py:201
  1019.7 109.6 %reduce-scatter.37.cloned.1.call-start = ((), (), s32[]{:S(2)}) async-start(), calls=%async_computation.31 | async-start | bytes 36864 | tf_op jit(solution)/shard_map/reduce_scatter | solution.py:218
  1022.7 150.4 %reduce-scatter.35.cloned.1.call-start = ((), (), s32[]{:S(2)}) async-start(), calls=%async_computation.30 | async-start | bytes 36864 | tf_op jit(solution)/shard_map/reduce_scatter | solution.py:218
  1024.1 214.9 %reduce-scatter.33.cloned.1.call-start = ((), (), s32[]{:S(2)}) async-start(), calls=%async_computation.29 | async-start | bytes 1179648 | tf_op jit(solution)/shard_map/reduce_scatter | solution.py:217
  1027.9 277.8 %reduce-scatter.31.cloned.1.call-start = ((), (), s32[]{:S(2)}) async-start(), calls=%async_computation.28 | async-start | bytes 1179648 | tf_op jit(solution)/shard_map/reduce_scatter | solution.py:217
  1066.6 309.8 %reduce-scatter.41.cloned.1.call-start = ((), (), s32[]{:S(2)}) async-start(), calls=%async_computation.33 | async-start | bytes 2359296 | tf_op jit(solution)/shard_map/reduce_scatter | solution.py:219
  1071.4 375.8 %reduce-scatter.39.cloned.1.call-start = ((), (), s32[]{:S(2)}) async-start(), calls=%async_computation.32 | async-start | bytes 2359296 | tf_op jit(solution)/shard_map/reduce_scatter | solution.py:219
  1077.2 440.3 %reduce-scatter.29.cloned.1.call-start = ((), (), s32[]{:S(2)}) async-start(), calls=%async_computation.27 | async-start | bytes 2359296 | tf_op jit(solution)/shard_map/reduce_scatter | solution.py:216
  1081.5 506.1 %reduce-scatter.27.cloned.1.call-start = ((), (), s32[]{:S(2)}) async-start(), calls=%async_computation.26 | async-start | bytes 2359296 | tf_op jit(solution)/shard_map/reduce_scatter | solution.py:216
  1103.4 554.4 %reduce-scatter.25.cloned.1.call-start = ((), (), s32[]{:S(2)}) async-start(), calls=%async_computation.25 | async-start | bytes 2359296 | tf_op jit(solution)/shard_map/reduce_scatter | solution.py:215
  1108.5 619.3 %reduce-scatter.23.cloned.1.call-start = ((), (), s32[]{:S(2)}) async-start(), calls=%async_computation.24 | async-start | bytes 2359296 | tf_op jit(solution)/shard_map/reduce_scatter | solution.py:215
  1112.8 668.0 %reduce-scatter.21.cloned.1.call-start = ((), (), s32[]{:S(2)}) async-start(), calls=%async_computation.22 | async-start | bytes 6553600 | tf_op jit(solution)/shard_map/reduce_scatter | solution.py:208
  1121.1 714.4 %reduce-scatter.17.cloned.1.call-start = ((), (), s32[]{:S(2)}) async-start(), calls=%async_computation.17 | async-start | bytes 6553600 | tf_op jit(solution)/shard_map/reduce_scatter | solution.py:150
  1128.1 652.7 %copy-start.20 = (bf16[320,1024]{1,0:T(8,128)(2,1)S(1)}, bf16[320,1024]{1,0:T(8,128)(2,1)}, u32[]{:S(2)}) copy-start(bf16[320,1024]{1,0:T(8,128)(2,1)} %param.29) | copy-start | bytes 1966084
  1128.1 652.7 %copy-start.90 = (f32[1,1024]{1,0:T(1,128)S(1)}, f32[1,1024]{1,0:T(1,128)}, u32[]{:S(2)}) copy-start(f32[1,1024]{1,0:T(1,128)} %copy-done.89) | copy-start | bytes 12292
  1128.2 652.7 %copy-start.97 = (f32[320]{0:T(512)S(1)}, f32[320]{0:T(512)}, u32[]{:S(2)}) copy-start(f32[320]{0:T(512)} %copy-done.96) | copy-start | bytes 3844
  1589.4 194.5 %copy-start.129 = (f32[1024]{0:T(1024)S(1)}, f32[1024]{0:T(1024)}, u32[]{:S(2)}) copy-start(f32[1024]{0:T(1024)} %get-tuple-element.1388) | copy-start | bytes 12292
  1589.4 246.1 %copy-start.6 = (f32[320,1024]{1,0:T(8,128)S(1)}, f32[320,1024]{1,0:T(8,128)}, u32[]{:S(2)}) copy-start(f32[320,1024]{1,0:T(8,128)} %copy-done.4) | copy-start | bytes 3932164
  1589.4 246.1 %copy-start.24 = (f32[320,1024]{1,0:T(8,128)S(1)}, f32[320,1024]{1,0:T(8,128)}, u32[]{:S(2)}) copy-start(f32[320,1024]{1,0:T(8,128)} %copy-done.23) | copy-start | bytes 3932164
  1589.4 246.1 %copy-start.88 = (f32[1,1024]{1,0:T(1,128)S(1)}, f32[1,1024]{1,0:T(1,128)}, u32[]{:S(2)}) copy-start(f32[1,1024]{1,0:T(1,128)} %copy-done.86) | copy-start | bytes 12292
  1589.4 246.1 %copy-start.95 = (f32[320]{0:T(512)S(1)}, f32[320]{0:T(512)}, u32[]{:S(2)}) copy-start(f32[320]{0:T(512)} %copy-done.93) | copy-start | bytes 3844
  1589.4 246.1 %copy-start.104 = (f32[320]{0:T(512)S(1)}, f32[320]{0:T(512)}, u32[]{:S(2)}) copy-start(f32[320]{0:T(512)} %copy-done.103) | copy-start | bytes 3844
  (263 other events, 2529.3 us)
Sparse Core Ops, SparseCore 0:
  11.8 28.2 all-gather.20
  42.8 40.2 all-gather.28
  85.8 39.0 all-gather.30
  127.3 38.3 all-gather.32
  186.7 50.3 reduce-scatter.14
  240.9 25.5 all-gather.22
  269.4 40.2 all-gather.34
  312.6 38.9 all-gather.36
  353.8 38.3 all-gather.38
  393.7 24.6 all-gather.24
  667.3 37.2 all-reduce.45
  707.1 51.4 reduce-scatter.18
  763.9 25.5 all-gather.26
  1019.8 40.0 all-reduce.47
  1063.4 53.4 reduce-scatter.36
  1120.5 52.5 reduce-scatter.34
  1176.3 62.5 reduce-scatter.32
  1243.2 62.4 reduce-scatter.30
  1309.2 67.1 reduce-scatter.40
  1379.8 67.3 reduce-scatter.38
  1450.7 66.6 reduce-scatter.28
  1521.0 66.5 reduce-scatter.26
  1591.1 66.6 reduce-scatter.24
  1661.2 66.4 reduce-scatter.22
  1730.3 50.4 reduce-scatter.20
  1783.4 52.0 reduce-scatter.16
where the time goes:
time: 1860 us; the launch traced here: 1850 us
  waiting for transfers between devices  770 us (41%)
  matrix products  404 us (22%)
  local copies, waits for them, and re-layouts  228 us (12%)
  blocking collectives  217 us (12%)
  other arithmetic  205 us (11%)
    dot_general x40, matrix products, span_step(): jnp.einsum('shij,sjhp->sihp', weights, inputs, precision=HIGHEST_PRECISION)  165 us
    reduce_scatter x2, waiting for transfers between devices, body(): lax.psum_scatter(g_down, 'dp', scatter_dimension=1, tiled=True)  140 us
    reduce_scatter x2, waiting for transfers between devices, body(): lax.psum_scatter(over_rows(gathered, x_low), 'dp', scatter_dimension=0, t...  139 us
    reduce_scatter x2, waiting for transfers between devices, body(): lax.psum_scatter(over_rows(gathered, z_low), 'dp', scatter_dimension=0, t...  138 us
    reduce_scatter x2, waiting for transfers between devices, body(): lax.psum_scatter(summed + project_back(dt_low, w_step), 'mp', scatter_dim...  101 us
    reduce_scatter x2, waiting for transfers between devices, body(): lax.psum_scatter(over_rows(gathered, bc_low), 'dp', scatter_dimension=0,...  94.5 us
    another operation x147, other arithmetic  73.8 us
    all_gather x2, blocking collectives, body(): lax.all_gather(w_bc[depth], 'dp', axis=0, tiled=True)  64.6 us
  transfers between devices with their start and end apart: 26, of which 17 were waited for; matrix products, arithmetic and copies ran while one was open for 24% of the time, Pallas kernels for 0%

commit v1 on v0

v1 whole, which is shorter than its diff:
```python
import functools

import jax
import jax.numpy as jnp
from jax import lax
from jax.experimental import pallas as pl
from jax.experimental.pallas import tpu as pltpu
from jax.sharding import PartitionSpec as P

INNER = 2048
HEADDIM = 64
STATE = 128
SPAN = 256
LEN = 1280
PAIR = 2 * HEADDIM
LANES = 128

epsilon = 1e-05
HIGHEST = lax.Precision.HIGHEST
F32 = jnp.float32
BF16 = jnp.bfloat16


def contract(left, right, dims):
    return lax.dot_general(left, right, (dims, ((), ())), preferred_element_type=F32)


NN = ((1,), (0,))
NT = ((1,), (1,))
TN = ((0,), (0,))


def causal_conv(values, kernel, offset):
    rows, width = values.shape
    taps = kernel.shape[0]
    seqs = values.reshape(rows // LEN, LEN, width)
    padded = jnp.pad(seqs, ((0, 0), (taps - 1, 0), (0, 0)))
    summed = offset + jnp.zeros_like(seqs)
    for tap in range(taps):
        summed = summed + padded[:, tap : tap + LEN, :] * kernel[tap]
    return jax.nn.silu(summed).reshape(rows, width)


def pair_masks():
    lane = lax.broadcasted_iota(jnp.int32, (1, PAIR), 1)
    first = lane < HEADDIM
    return first, jnp.logical_not(first)


def lower_mask():
    row = lax.broadcasted_iota(jnp.int32, (SPAN, SPAN), 0)
    col = lax.broadcasted_iota(jnp.int32, (SPAN, SPAN), 1)
    return row >= col


def scan_forward(heads, x_ref, b_ref, c_ref, dt_ref, dtt_ref, l_ref, lt_ref, skip_ref, y_ref, h_ref, state):
    @pl.when(pl.program_id(1) == 0)
    def _():
        state[...] = jnp.zeros_like(state)

    h_ref[0] = state[...]
    keys = b_ref[...].astype(BF16)
    reads = c_ref[...].astype(BF16)
    scores = contract(reads, keys, NT)
    lower = lower_mask()
    masks = pair_masks()
    for pair in range(heads // 2):
        lanes = slice(pair * PAIR, (pair + 1) * PAIR)
        x = x_ref[:, lanes]
        held = state[:, lanes]
        inner = None
        grown, tails, shrink = [], [], []
        for k in range(2):
            h = 2 * pair + k
            l_col = l_ref[:, h : h + 1]
            last = l_ref[SPAN - 1 : SPAN, h : h + 1]
            decay = jnp.exp(jnp.where(lower, l_col - lt_ref[h : h + 1, :], -1e30))
            weights = (scores * decay * dtt_ref[h : h + 1, :]).astype(BF16)
            part = contract(weights, jnp.where(masks[k], x, 0.0).astype(BF16), NN)
            inner = part if inner is None else inner + part
            grown.append(jnp.exp(l_col))
            tails.append(jnp.exp(last - l_col) * dt_ref[:, h : h + 1])
            shrink.append(jnp.exp(last))
        carried = contract(reads, held.astype(BF16), NN) * jnp.where(masks[0], grown[0], grown[1])
        y_ref[:, lanes] = inner + carried + x * skip_ref[:, lanes]
        scaled = (x * jnp.where(masks[0], tails[0], tails[1])).astype(BF16)
        state[:, lanes] = held * jnp.where(masks[0], shrink[0], shrink[1]) + contract(keys, scaled, TN)


def scan_backward(
    heads,
    x_ref, b_ref, c_ref, dt_ref, dtt_ref, l_ref, lt_ref, skip_ref, h_ref, dy_ref,
    dx_ref, db_ref, dc_ref, dl_ref, ddt_ref, col_ref, xdy_ref,
    d_state,
):
    @pl.when(pl.program_id(1) == 0)
    def _():
        d_state[...] = jnp.zeros_like(d_state)

    keys = b_ref[...].astype(BF16)
    reads = c_ref[...].astype(BF16)
    scores = contract(reads, keys, NT)
    lower = lower_mask()
    masks = pair_masks()
    head_lane = lax.broadcasted_iota(jnp.int32, (1, heads), 1)
    is_last = lax.broadcasted_iota(jnp.int32, (SPAN, 1), 0) == SPAN - 1
    d_scores = jnp.zeros((SPAN, SPAN), F32)
    d_keys = jnp.zeros((SPAN, STATE), F32)
    d_reads = jnp.zeros((SPAN, STATE), F32)
    d_logs = jnp.zeros((SPAN, heads), F32)
    d_steps = jnp.zeros((SPAN, heads), F32)
    x_dy = jnp.zeros((SPAN, heads), F32)
    for pair in range(heads // 2):
        lanes = slice(pair * PAIR, (pair + 1) * PAIR)
        x = x_ref[:, lanes]
        dy = dy_ref[:, lanes]
        held = h_ref[0, :, lanes]
        d_held = d_state[:, lanes]
        l_cols = [l_ref[:, 2 * pair + k : 2 * pair + k + 1] for k in range(2)]
        lasts = [l_ref[SPAN - 1 : SPAN, 2 * pair + k : 2 * pair + k + 1] for k in range(2)]
        dt_cols = [dt_ref[:, 2 * pair + k : 2 * pair + k + 1] for k in range(2)]
        rests = [jnp.exp(lasts[k] - l_cols[k]) for k in range(2)]
        shrink = [jnp.exp(lasts[k]) for k in range(2)]
        grown = jnp.where(masks[0], jnp.exp(l_cols[0]), jnp.exp(l_cols[1]))
        tails = jnp.where(masks[0], rests[0] * dt_cols[0], rests[1] * dt_cols[1])
        x_low = x.astype(BF16)
        held_low = held.astype(BF16)
        d_held_low = d_held.astype(BF16)
        outer = dy * grown
        outer_low = outer.astype(BF16)
        from_logs = outer * contract(reads, held_low, NN)
        d_reads = d_reads + contract(outer_low, held_low, NT)
        carried = contract(keys, d_held_low, NN)
        from_tails = x * carried
        d_keys = d_keys + contract((x * tails).astype(BF16), d_held_low, NT)
        x_times_dy = x * dy
        d_x = tails * carried + skip_ref[:, lanes] * dy
        kept = jnp.sum(held * d_held, axis=0, keepdims=True)
        for k in range(2):
            h = 2 * pair + k
            step_row = dtt_ref[h : h + 1, :]
            decay = jnp.exp(jnp.where(lower, l_cols[k] - lt_ref[h : h + 1, :], -1e30))
            scored = scores * decay
            dy_low = jnp.where(masks[k], dy, 0.0).astype(BF16)
            d_weights = contract(dy_low, x_low, NT)
            d_x = d_x + contract((scored * step_row).astype(BF16), dy_low, TN)
            product = d_weights * scored
            d_scores = d_scores + d_weights * decay * step_row
            col_ref[0, h : h + 1, :] = jnp.sum(product, axis=0, keepdims=True)
            row_sum = jnp.sum(product * step_row, axis=1, keepdims=True)
            log_sum = jnp.sum(jnp.where(masks[k], from_logs, 0.0), axis=1, keepdims=True)
            tail_sum = jnp.sum(jnp.where(masks[k], from_tails, 0.0), axis=1, keepdims=True)
            skip_sum = jnp.sum(jnp.where(masks[k], x_times_dy, 0.0), axis=1, keepdims=True)
            step_part = tail_sum * rests[k]
            tail_part = step_part * dt_cols[k]
            ending = shrink[k] * jnp.sum(jnp.where(masks[k], kept, 0.0), axis=1, keepdims=True) + jnp.sum(
                tail_part, axis=0, keepdims=True
            )
            log_part = log_sum + row_sum - tail_part + jnp.where(is_last, ending, 0.0)
            here = head_lane == h
            d_logs = jnp.where(here, log_part, d_logs)
            d_steps = jnp.where(here, step_part, d_steps)
            x_dy = jnp.where(here, skip_sum, x_dy)
        dx_ref[:, lanes] = d_x
        d_state[:, lanes] = d_held * jnp.where(masks[0], shrink[0], shrink[1]) + contract(reads, outer_low, TN)
    d_scores_low = d_scores.astype(BF16)
    dc_ref[...] = d_reads + contract(d_scores_low, keys, NN)
    db_ref[...] = d_keys + contract(d_scores_low, reads, TN)
    dl_ref[...] = d_logs
    ddt_ref[...] = d_steps
    xdy_ref[...] = x_dy


def scan_specs(rows, width, heads, backward):
    count = LEN // SPAN

    def at(seq, step):
        return seq * count + ((count - 1 - step) if backward else step)

    def rowwise(columns, column=0):
        return pl.BlockSpec((SPAN, columns), lambda s, i: (at(s, i), column))

    def stacked(first, second):
        return pl.BlockSpec((1, first, second), lambda s, i: (at(s, i), 0, 0))

    across = pl.BlockSpec((heads, SPAN), lambda s, i: (0, at(s, i)))
    whole = pl.BlockSpec((1, width), lambda s, i: (0, 0))
    operands = [rowwise(width), rowwise(STATE, 0), rowwise(STATE, 1), rowwise(heads), across, rowwise(heads), across, whole]
    return operands, rowwise, stacked, (rows // LEN, count)


PARAMS = pltpu.CompilerParams(
    dimension_semantics=("arbitrary", "arbitrary"), vmem_limit_bytes=40 * 1024 * 1024
)


def run_forward(x, bc, steps, logs, skip):
    rows, width = x.shape
    heads = steps.shape[1]
    operands, rowwise, stacked, grid = scan_specs(rows, width, heads, False)
    blocks = rows // SPAN
    return pl.pallas_call(
        functools.partial(scan_forward, heads),
        grid=grid,
        in_specs=operands,
        out_specs=[rowwise(width), stacked(STATE, width)],
        out_shape=[
            jax.ShapeDtypeStruct((rows, width), F32),
            jax.ShapeDtypeStruct((blocks, STATE, width), F32),
        ],
        scratch_shapes=[pltpu.VMEM((STATE, width), F32)],
        compiler_params=PARAMS,
        cost_estimate=pl.CostEstimate(
            flops=blocks * heads * 4 * SPAN * SPAN * PAIR * 4, bytes_accessed=rows * width * 10, transcendentals=blocks * heads * SPAN * SPAN
        ),
        name="scan_forward",
    )(x, bc, bc, steps, steps.T, logs, logs.T, skip)


def run_backward(x, bc, steps, logs, skip, states, d_y):
    rows, width = x.shape
    heads = steps.shape[1]
    operands, rowwise, stacked, grid = scan_specs(rows, width, heads, True)
    blocks = rows // SPAN
    return pl.pallas_call(
        functools.partial(scan_backward, heads),
        grid=grid,
        in_specs=operands + [stacked(STATE, width), rowwise(width)],
        out_specs=[
            rowwise(width), rowwise(STATE), rowwise(STATE), rowwise(heads), rowwise(heads), stacked(heads, SPAN), rowwise(heads),
        ],
        out_shape=[
            jax.ShapeDtypeStruct((rows, width), F32),
            jax.ShapeDtypeStruct((rows, STATE), F32),
            jax.ShapeDtypeStruct((rows, STATE), F32),
            jax.ShapeDtypeStruct((rows, heads), F32),
            jax.ShapeDtypeStruct((rows, heads), F32),
            jax.ShapeDtypeStruct((blocks, heads, SPAN), F32),
            jax.ShapeDtypeStruct((rows, heads), F32),
        ],
        scratch_shapes=[pltpu.VMEM((STATE, width), F32)],
        compiler_params=PARAMS,
        cost_estimate=pl.CostEstimate(
            flops=blocks * heads * 12 * SPAN * SPAN * PAIR * 4, bytes_accessed=rows * width * 20, transcendentals=blocks * heads * SPAN * SPAN
        ),
        name="scan_backward",
    )(x, bc, bc, steps, steps.T, logs, logs.T, skip, states, d_y)


def block_sums(values, reverse):
    rows, heads = values.shape
    lower = jnp.tril(jnp.ones((SPAN, SPAN), F32))
    blocks = values.reshape(rows // SPAN, SPAN, heads)
    form = "ij,cih->cjh" if reverse else "ij,cjh->cih"
    return jnp.einsum(form, lower, blocks, precision=HIGHEST).reshape(rows, heads)


def swap_mp(value, bit, size):
    return lax.ppermute(value, "mp", [(i, i ^ bit) for i in range(size)])


def gather_mp(value):
    size = lax.axis_size("mp")
    if size != 4:
        return lax.all_gather(value, "mp", axis=0, tiled=True)
    chip, core = lax.axis_index("mp") // 2, lax.axis_index("mp") % 2
    far = swap_mp(value, 2, size)
    column = jnp.stack([jnp.where(chip == 0, value, far), jnp.where(chip == 0, far, value)])
    near = swap_mp(column, 1, size)
    both = jnp.stack([jnp.where(core == 0, column, near), jnp.where(core == 0, near, column)], axis=1)
    return both.reshape((size * value.shape[0],) + value.shape[1:])


def scatter_mp(value):
    size = lax.axis_size("mp")
    if size != 4:
        return lax.psum_scatter(value, "mp", scatter_dimension=0, tiled=True)
    chip, core = lax.axis_index("mp") // 2, lax.axis_index("mp") % 2
    parts = value.reshape(2, 2, value.shape[0] // size, value.shape[1])
    near = swap_mp(lax.dynamic_index_in_dim(parts, 1 - core, 1, False).astype(BF16), 1, size)
    column = lax.dynamic_index_in_dim(parts, core, 1, False) + near.astype(F32)
    far = swap_mp(lax.dynamic_index_in_dim(column, 1 - chip, 0, False).astype(BF16), 2, size)
    return lax.dynamic_index_in_dim(column, chip, 0, False) + far.astype(F32)


def sum_all(value, axis):
    size = lax.axis_size(axis)
    bit = 1
    while bit < size:
        value = value + lax.ppermute(value, axis, [(i, i ^ bit) for i in range(size)])
        bit *= 2
    return value


def reduce_line(parts, place, size, device):
    own = lax.dynamic_index_in_dim(parts, place, 0, False)
    for way in (1, -1):
        along = place if way == 1 else size - 1 - place
        sent = None
        for step in range(size - 1):
            target = jnp.clip(place + way * (size - 1 - step), 0, size - 1)
            part = lax.dynamic_index_in_dim(parts, target, 0, False)
            if sent is not None:
                part = part + sent.astype(F32)
            pairs = []
            for row in range(step + 1):
                here = row if way == 1 else size - 1 - row
                pairs += device(here, here + way)
            sent = lax.ppermute(part.astype(BF16), "dp", pairs)
        own = own + sent.astype(F32)
    return own


def scatter_dp(value):
    size = lax.axis_size("dp")
    if size != 8:
        return lax.psum_scatter(value, "dp", scatter_dimension=0, tiled=True)
    outer, inner = 4, 2
    parts = value.reshape(outer, inner, value.shape[0] // size, value.shape[1])
    index = lax.axis_index("dp")
    column = reduce_line(
        parts, index // inner, outer, lambda a, b: [(a * inner + i, b * inner + i) for i in range(inner)]
    )
    return reduce_line(
        column, index % inner, inner, lambda a, b: [(o * inner + a, o * inner + b) for o in range(outer)]
    )


def body(
    tokens, cotangent, in_gain, w_z, w_x, w_bc, w_dt, conv_x_w, conv_x_b, conv_bc_w, conv_bc_b, dt_bias, a_log, dskip, norm_gain, w_out,
):
    layers = w_z.shape[0]
    width = w_z.shape[2]
    heads = w_dt.shape[2]
    pair = w_bc.shape[2]
    inputs = 2 * width + pair + LANES
    pad_heads = ((0, 0), (0, LANES - heads))
    packed = []
    for depth in range(layers):
        own = jnp.concatenate(
            [w_z[depth], w_x[depth], w_bc[depth], jnp.pad(w_dt[depth], pad_heads), w_out[depth].T], axis=1
        )
        packed.append(
            tuple(lax.all_gather(part, "dp", axis=0, tiled=True) for part in (own[:, :inputs], own[:, inputs:]))
        )

    current = tokens.astype(F32)
    saved = []
    for depth in range(layers):
        w_in, w_down = packed[depth]
        scale = lax.rsqrt(jnp.mean(current * current, axis=-1, keepdims=True) + epsilon)
        normed = (current * scale * in_gain[depth]).astype(BF16)
        gathered = gather_mp(normed)
        raw = contract(gathered, w_in, NN)
        z_val = raw[:, :width]
        x_raw = raw[:, width : 2 * width]
        bc_raw = raw[:, 2 * width : 2 * width + pair]
        dt_in = raw[:, 2 * width + pair : 2 * width + pair + heads] + dt_bias[depth]
        x_act = causal_conv(x_raw, conv_x_w[depth], conv_x_b[depth])
        bc_act = causal_conv(bc_raw, conv_bc_w[depth], conv_bc_b[depth])
        steps = jax.nn.softplus(dt_in)
        rate = -jnp.exp(a_log[depth])
        logs = block_sums(steps * rate, False)
        skip = jnp.repeat(dskip[depth], HEADDIM)[None, :]
        mixed_y, states = run_forward(x_act, bc_act, steps, logs, skip)
        gated = mixed_y * jax.nn.silu(z_val)
        squares = lax.psum(jnp.sum(gated * gated, axis=-1), "mp")
        ratio = lax.rsqrt(squares / INNER + epsilon)[:, None]
        mixed = (gated * ratio * norm_gain[depth]).astype(BF16)
        branch = scatter_mp(contract(mixed, w_down, NT))
        saved.append((current, scale, gathered, raw, dt_in, x_act, bc_act, steps, rate, logs, skip, mixed_y, states, ratio, mixed))
        current = current + branch

    result = current
    gradient = cotangent.astype(F32)
    list_proj, list_own, list_shared = ([], [], [])
    for depth in reversed(range(layers)):
        current, scale, gathered, raw, dt_in, x_act, bc_act, steps, rate, logs, skip, mixed_y, states, ratio, mixed = saved[depth]
        w_in, w_down = packed[depth]
        z_val = raw[:, :width]
        x_raw = raw[:, width : 2 * width]
        bc_raw = raw[:, 2 * width : 2 * width + pair]
        grad_rows = gather_mp(gradient.astype(BF16))
        d_mixed = contract(grad_rows, w_down, NN)
        sigmoid_z = jax.nn.sigmoid(z_val)
        gate_act = z_val * sigmoid_z
        gated = mixed_y * gate_act
        weighted = d_mixed * norm_gain[depth]
        products = lax.psum(jnp.sum(weighted * gated, axis=-1), "mp")
        g_gain_norm = jnp.sum(d_mixed * gated * ratio, axis=0)
        d_gated = ratio * weighted - gated * ratio * ratio * ratio * (products / INNER)[:, None]
        d_y = d_gated * gate_act
        d_z = d_gated * mixed_y * sigmoid_z * (1.0 + z_val * (1.0 - sigmoid_z))
        z_low = d_z.astype(BF16)
        early = scatter_dp(jnp.concatenate([contract(gathered, z_low, TN), contract(grad_rows, mixed, TN)], axis=1))
        d_x, d_keys, d_reads, d_logs, d_steps, columns, x_dy = run_backward(x_act, bc_act, steps, logs, skip, states, d_y)
        columns = jnp.swapaxes(columns, 1, 2).reshape(steps.shape)
        d_ramps = block_sums(d_logs - steps * columns, True)
        g_alog = jnp.sum(steps * d_ramps, axis=0) * rate
        d_dtr = (d_steps + columns + rate * d_ramps) * jax.nn.sigmoid(dt_in)
        g_dtb = jnp.sum(d_dtr, axis=0)
        g_skip = jnp.sum(x_dy, axis=0)
        _, x_pull = jax.vjp(causal_conv, x_raw, conv_x_w[depth], conv_x_b[depth])
        _, bc_pull = jax.vjp(causal_conv, bc_raw, conv_bc_w[depth], conv_bc_b[depth])
        d_xr, g_cxw, g_cxb = x_pull(d_x)
        d_bcr, g_cbw, g_cbb = bc_pull(jnp.concatenate([d_keys, d_reads], axis=1))
        d_low = jnp.concatenate(
            [d_xr.astype(BF16), d_bcr.astype(BF16), jnp.pad(d_dtr.astype(BF16), pad_heads)], axis=1
        )
        d_normed = scatter_mp(contract(z_low, w_in[:, :width], NT) + contract(d_low, w_in[:, width:], NT))
        late = scatter_dp(contract(gathered, d_low, TN))
        list_proj.append((early[:, :width], late[:, :width], late[:, width : width + pair], late[:, width + pair : width + pair + heads], early[:, width:].T))
        gained = d_normed * in_gain[depth]
        g_gain_in = jnp.sum(d_normed * current * scale, axis=0)
        gradient = (
            gradient
            + scale * gained
            - current * scale * scale * scale * jnp.mean(gained * current, axis=-1, keepdims=True)
        )
        list_own.append((g_cxw, g_cxb, g_dtb, g_alog, g_skip, g_gain_norm))
        list_shared.append((g_cbw, g_cbb, g_gain_in))
    proj = [jnp.stack([entry[i] for entry in list_proj[::-1]]) for i in range(5)]
    own = [jnp.stack([entry[i] for entry in list_own[::-1]]) for i in range(6)]
    shared = [jnp.stack([entry[i] for entry in list_shared[::-1]]) for i in range(3)]
    sums = sum_all(jnp.concatenate([value.reshape(-1) for value in own + shared]), "dp")
    kept = sum(value.size for value in own)
    pieces, place = [], 0
    for value in own:
        pieces.append(sums[place : place + value.size].reshape(value.shape))
        place += value.size
    g_bc = proj[2]
    across = sum_all(jnp.concatenate([sums[kept:], g_bc.reshape(-1)]), "mp")
    place = 0
    for value in shared + [g_bc]:
        pieces.append(across[place : place + value.size].reshape(value.shape))
        place += value.size
    g_cxw, g_cxb, g_dtb, g_alog, g_skip, g_gain_norm, g_cbw, g_cbb, g_gain_in, g_bc = pieces
    return (
        result,
        gradient,
        g_gain_in,
        proj[0],
        proj[1],
        g_bc,
        proj[3],
        g_cxw,
        g_cxb,
        g_cbw,
        g_cbb,
        g_dtb,
        g_alog,
        g_skip,
        g_gain_norm,
        proj[4],
    )


def solution(mesh):
    placed = (
        P(("dp", "mp"), None),
        P(("dp", "mp"), None),
        P(),
        P(None, "dp", "mp"),
        P(None, "dp", "mp"),
        P(None, "dp", None),
        P(None, "dp", "mp"),
        P(None, None, "mp"),
        P(None, "mp"),
        P(),
        P(),
        P(None, "mp"),
        P(None, "mp"),
        P(None, "mp"),
        P(None, "mp"),
        P(None, "mp", "dp"),
    )
    return jax.shard_map(
        body,
        mesh=mesh,
        in_specs=placed,
        out_specs=placed[:1] * 2 + placed[2:],
        check_vma=False,
    )
```

time: 1860 us -> 670 us (0.36)
  waiting for transfers between devices: 770 us -> 166 us
  matrix products: 404 us -> 61.3 us
  blocking collectives: 217 us -> 26.5 us
  local copies, waits for them, and re-layouts: 228 us -> 122 us
  starting transfers between devices: 2.26 us -> 99.4 us
  other arithmetic: 205 us -> 111 us
  Pallas kernels: 0 us -> 56.5 us
    reduce_scatter x14 -> x0, waiting for transfers between devices: 717 us -> none  [the longest x2 140 us: body(): lax.psum_scatter(g_down, 'dp', scatter_dimension=1, tiled=True)]
    dot_general x180 -> x20, matrix products: 387 us -> 61.3 us  [the longest x16 60.1 us: contract(): lax.dot_general(left, right, (dims, ((), ())), preferred_element_type=F32)]
    ppermute x0 -> x53, waiting for transfers between devices: none -> 127 us  [the longest x16 78.1 us: swap_mp(): return lax.ppermute(value, 'mp', [(i, i ^ bit) for i in range(size)])]
    all_gather x4 -> x0, blocking collectives: 117 us -> none  [the longest x2 64.6 us: body(): lax.all_gather(w_bc[depth], 'dp', axis=0, tiled=True)]
    ppermute x0 -> x53, starting transfers between devices: none -> 98.8 us  [the longest x32 83.2 us: reduce_line(): sent = lax.ppermute(part.astype(BF16), 'dp', pairs)]
    psum x2 -> x0, blocking collectives: 76.4 us -> none  [the longest x1 39.7 us: body(): gain_sums = lax.psum(jnp.stack(list_in_gain), ('dp', 'mp'))]
    another operation x172 -> x28, other arithmetic: 82.7 us -> 15.2 us  [the longest x8 7.32 us: gather_mp(): jnp.stack([jnp.where(core == 0, column, near), jnp.where(core == 0, near,...]
    pallas_call x0 -> x4, Pallas kernels: none -> 56.5 us  [the longest x2 43.6 us: run_backward(): pl.pallas_call(functools.partial(scan_backward, heads), grid=grid, in_spe...]
  transfers between devices with their start and end apart: 26 -> 57, of which waited for: 17 -> 22; matrix products, arithmetic and copies ran while one was open for 24% -> 25% of each run, Pallas kernels for 0% -> 2%
where the time goes in v1:
time: 670 us; the launch traced here: 660 us
  waiting for transfers between devices  166 us (25%)
  local copies, waits for them, and re-layouts  122 us (18%)
  other arithmetic  111 us (17%)
  starting transfers between devices  99.4 us (15%)
  matrix products  61.3 us (9%)
  Pallas kernels  56.5 us (8%)
  blocking collectives  26.5 us (4%)
  between operations  17.1 us (3%)
    ppermute x32, starting transfers between devices, reduce_line(): sent = lax.ppermute(part.astype(BF16), 'dp', pairs)  83.2 us
    ppermute x16, waiting for transfers between devices, swap_mp(): return lax.ppermute(value, 'mp', [(i, i ^ bit) for i in range(size)])  78.1 us
    dot_general x16, matrix products, contract(): lax.dot_general(left, right, (dims, ((), ())), preferred_element_type=F32)  60.1 us
    unnamed x348, local copies, waits for them, and re-layouts  49.1 us
    pallas_call x2, Pallas kernels, run_backward(): pl.pallas_call(functools.partial(scan_backward, heads), grid=grid, in_spe...  43.6 us
    all_gather x4, waiting for transfers between devices, body(): lax.all_gather(part, 'dp', axis=0, tiled=True)  38.2 us
    ppermute x32, waiting for transfers between devices, reduce_line(): sent = lax.ppermute(part.astype(BF16), 'dp', pairs)  37.7 us
    reshape x4, other arithmetic, causal_conv(): return jax.nn.silu(summed).reshape(rows, width)  16.6 us
  transfers between devices with their start and end apart: 57, of which 22 were waited for; matrix products, arithmetic and copies ran while one was open for 25% of the time, Pallas kernels for 2%

profile of v1, /device:TPU:0, one launch (start us, length us, event | category | flops | bytes accessed | tf_op | source)
XLA Modules:
  0.0 659.6 jit_solution(1168764583873483860)
XLA Ops:
  17.5 12.4 %collective-permute-done = bf16[320,1024]{1,0:T(8,128)(2,1)S(1)} collective-permute-done((bf16[320,1024]{1,0:T(8,128)(2,1)S(1)}, bf16[320,1024]{1,0:T(8,128)(2,1)S(1)}, u32[]{:S(2)}, u32[]{:S(2)}) %collective-permute-start) | collective-permute-done | bytes 655392 | tf_op jit(solution)/shard_map/ppermute | solution.py:259
  36.0 36.2 %all-gather.5.cloned.1.call-done = bf16[1024,1408]{1,0:T(8,128)(2,1)} async-done(((bf16[128,1408]{1,0:T(8,128)(2,1)}), bf16[1024,1408]{1,0:T(8,128)(2,1)}) %all-gather.5.cloned.1.call-update) | async-done | bytes 2883600 | tf_op jit(solution)/shard_map/all_gather | solution.py:344
  72.1 6.9 %fusion.168 = f32[1280,1408]{1,0:T(8,128)S(1)} fusion(bf16[1280,1024]{1,0:T(8,128)(2,1)} %bitcast.565, bf16[1024,1408]{1,0:T(8,128)(2,1)} %all-gather.5.cloned.1.call-done), kind=kOutput, calls=%fused_computation.419 | convolution fusion | flops 3690987520 | bytes 12713984 | tf_op jit(solution)/shard_map/dot_general | solution.py:25
  84.7 6.3 multiply_bitcast_fusion.1
  95.2 6.5 scan_forward.2
  103.5 6.7 %psum.28 = f32[1280]{0:T(1024)} all-reduce(f32[1280]{0:T(1024)S(1)} %get-tuple-element.148), channel_id=1, replica_groups=mesh['dp'=8,'mp'=4] {'mp'}, use_global_device_ids=true, to_apply=%region_2.3 | all-reduce | flops 1280 | bytes 10240 | tf_op jit(solution)/shard_map/psum | solution.py:367
  127.1 15.9 %collective-permute-done.3 = bf16[320,1024]{1,0:T(8,128)(2,1)} collective-permute-done((bf16[320,1024]{1,0:T(8,128)(2,1)}, bf16[320,1024]{1,0:T(8,128)(2,1)}, u32[]{:S(2)}, u32[]{:S(2)}) %collective-permute-start.3) | collective-permute-done | bytes 655392 | tf_op jit(solution)/shard_map/ppermute | solution.py:259
  146.2 10.8 %collective-permute-done.8 = bf16[320,1024]{1,0:T(8,128)(2,1)} collective-permute-done((bf16[320,1024]{1,0:T(8,128)(2,1)}, bf16[320,1024]{1,0:T(8,128)(2,1)}, u32[]{:S(2)}, u32[]{:S(2)}) %collective-permute-start.8) | collective-permute-done | bytes 655392 | tf_op jit(solution)/shard_map/ppermute | solution.py:259
  158.6 11.5 %collective-permute-done.4 = bf16[320,1024]{1,0:T(8,128)(2,1)S(1)} collective-permute-done((bf16[320,1024]{1,0:T(8,128)(2,1)S(1)}, bf16[320,1024]{1,0:T(8,128)(2,1)S(1)}, u32[]{:S(2)}, u32[]{:S(2)}) %collective-permute-start.4) | collective-permute-done | bytes 655392 | tf_op jit(solution)/shard_map/ppermute | solution.py:259
  182.2 7.0 %fusion.169 = f32[1280,1408]{1,0:T(8,128)S(1)} fusion(bf16[1280,1024]{1,0:T(8,128)(2,1)S(1)} %bitcast.568, bf16[1024,1408]{1,0:T(8,128)(2,1)} %all-gather.9.cloned.1.call-done), kind=kOutput, calls=%fused_computation.420 | convolution fusion | flops 3690987520 | bytes 12713984 | tf_op jit(solution)/shard_map/dot_general | solution.py:25
  193.8 4.7 multiply_bitcast_fusion
  208.0 6.4 scan_forward.3
  214.5 4.5 multiply_reduce_fusion.12
  219.0 7.5 %psum.29 = f32[1280]{0:T(1024)S(1)} all-reduce(f32[1280]{0:T(1024)S(1)} %get-tuple-element.138), channel_id=1, replica_groups=mesh['dp'=8,'mp'=4] {'mp'}, use_global_device_ids=true, to_apply=%region_5.6 | all-reduce | flops 1280 | bytes 10240 | tf_op jit(solution)/shard_map/psum | solution.py:367
  226.5 5.6 fusion.148
  232.1 6.8 %multiply_reduce_fusion = (f32[512]{0:T(512)}, f32[1280]{0:T(1024)S(1)}, f32[1280,512]{1,0:T(8,128)}) fusion(f32[1280,512]{1,0:T(8,128)} %get-tuple-element.139, f32[1280]{0:T(1024)S(1)} %add_rsqrt_fusion, f32[512]{0:T(512)S(1)} %bitcast.604, bf16[1280,1024]{1,0:T(8,128)(2,1)} %bitcast.573, bf16[1024,512]{0,1:T(8,128)(2,1)} %all-gather.11.cloned.1.call-done), kind=kOutput, calls=%fused_computation.39 | convolution fusion | flops 1346107648 | bytes 8927232 | tf_op jit(solution)/shard_map/dot_general | solution.py:25
  238.9 6.0 psum.30
  244.9 5.6 multiply_convert_fusion.1
  251.5 21.8 %scan_backward.2 = (f32[1280,512]{1,0:T(8,128)S(1)}, f32[1280,128]{1,0:T(8,128)S(1)}, f32[1280,128]{1,0:T(8,128)S(1)}, f32[1280,8]{1,0:T(8,128)S(1)}, f32[1280,8...) custom-call(f32[1280,512]{1,0:T(8,128)S(1)} %copy-done.5, f32[1280,256]{1,0:T(8,128)S(1)} %copy-done.9, ...), custom_call_target="tpu_custom_call" | custom-call | flops 16106127360 | bytes 13107200 | tf_op jit(solution)/shard_map/scan_backward/pallas_call | solution.py:225
  281.2 4.9 multiply_reduce_fusion.17
  288.7 3.8 multiply_reduce_fusion.4
  315.9 5.2 fusion.12
  330.6 7.0 %reshape.512 = f32[4,2,128,1024]{2,1,0,3:T(2,128)} reshape(f32[1024,1024]{0,1:T(8,128)} %pad_maximum_fusion.1) | data formatting | bytes 8388608 | tf_op jit(solution)/shard_map/reshape | solution.py:319
  347.9 9.6 %collective-permute-done.45 = bf16[2,128,1024]{1,2,0:T(8,128)(2,1)S(1)} collective-permute-done((bf16[2,128,1024]{1,2,0:T(8,128)(2,1)S(1)}, bf16[2,128,1024]{1,2,0:T(8,128)(2,1)S(1)}, u32[]{:S(2)}, u32[]{:S(2)}) %collective-permute-start.45) | collective-permute-done | bytes 524320 | tf_op jit(solution)/shard_map/ppermute | solution.py:309
  358.3 5.3 collective-permute-start.46
  369.3 7.8 %collective-permute-start.29 = (bf16[2,128,896]{2,1,0:T(8,128)(2,1)S(1)}, bf16[2,128,896]{2,1,0:T(8,128)(2,1)S(1)}, u32[]{:S(2)}, u32[]{:S(2)}) collective-permute-start(bf16[2,128,896]{2,1,0:T(8,128)(2,1)S(1)} %get-tuple-element.178), channel_id=1, source_target_pairs={{0,8},{4,12},{8,16},{12,20},{16,24},{20,28},{1,9},{5,13},{9,17},{1... | collective-permute-start | bytes 1376264 | tf_op jit(solution)/shard_map/ppermute | solution.py:309
  380.0 5.3 collective-permute-start.47
  391.6 13.6 %collective-permute-done.11 = bf16[320,1024]{1,0:T(8,128)(2,1)S(1)} collective-permute-done((bf16[320,1024]{1,0:T(8,128)(2,1)S(1)}, bf16[320,1024]{1,0:T(8,128)(2,1)S(1)}, u32[]{:S(2)}, u32[]{:S(2)}) %collective-permute-start.11) | collective-permute-done | bytes 655392 | tf_op jit(solution)/shard_map/ppermute | solution.py:259
  407.5 9.8 %collective-permute-done.7 = bf16[320,1024]{1,0:T(8,128)(2,1)S(1)} collective-permute-done((bf16[320,1024]{1,0:T(8,128)(2,1)S(1)}, bf16[320,1024]{1,0:T(8,128)(2,1)S(1)}, u32[]{:S(2)}, u32[]{:S(2)}) %collective-permute-start.7) | collective-permute-done | bytes 655392 | tf_op jit(solution)/shard_map/ppermute | solution.py:259
  422.4 4.6 collective-permute-start.51
  428.5 4.6 collective-permute-start.33
  448.8 6.3 psum.31
  455.2 5.7 multiply_convert_fusion
  461.8 21.8 %scan_backward.3 = (f32[1280,512]{1,0:T(8,128)S(1)}, f32[1280,128]{1,0:T(8,128)S(1)}, f32[1280,128]{1,0:T(8,128)S(1)}, f32[1280,8]{1,0:T(8,128)S(1)}, f32[1280,8...) custom-call(f32[1280,512]{1,0:T(8,128)S(1)} %copy-done.3, f32[1280,256]{1,0:T(8,128)S(1)} %copy-done.7, ...), custom_call_target="tpu_custom_call" | custom-call | flops 16106127360 | bytes 13107200 | tf_op jit(solution)/shard_map/scan_backward/pallas_call | solution.py:225
  491.0 4.2 multiply_reduce_fusion.21
  522.1 4.1 collective-permute-start.19
  527.9 4.1 pad_maximum_fusion
  532.0 6.6 %reshape.511 = f32[4,2,128,1024]{2,1,0,3:T(2,128)} reshape(f32[1024,1024]{0,1:T(8,128)} %pad_maximum_fusion) | data formatting | bytes 8388608 | tf_op jit(solution)/shard_map/reshape | solution.py:319
  554.4 5.7 collective-permute-done.37
  560.2 4.7 collective-permute-start.38
  564.9 5.0 collective-permute-done.20
  571.9 5.0 collective-permute-start.21
  581.3 4.4 collective-permute-start.39
  592.1 9.0 %collective-permute-done.39 = bf16[2,128,1024]{1,2,0:T(8,128)(2,1)S(1)} collective-permute-done((bf16[2,128,1024]{1,2,0:T(8,128)(2,1)S(1)}, bf16[2,128,1024]{1,2,0:T(8,128)(2,1)S(1)}, u32[]{:S(2)}, u32[]{:S(2)}) %collective-permute-start.39) | collective-permute-done | bytes 524320 | tf_op jit(solution)/shard_map/ppermute | solution.py:309
  602.6 4.7 collective-permute-start.43
  609.7 6.0 collective-permute-start.25
  623.8 4.0 collective-permute-done.16
  635.0 4.0 collective-permute-done.18
  (650 shorter events, 266.8 us)
Async XLA Ops:
  7.2 64.9 %all-gather.5.cloned.1.call-start = ((), (), s32[]{:S(2)}) async-start(), calls=%async_computation | async-start | bytes 3244032 | tf_op jit(solution)/shard_map/all_gather | solution.py:344
  11.6 101.3 %all-gather.7.cloned.1.call-start = ((), (), s32[]{:S(2)}) async-start(), calls=%async_computation.1 | async-start | bytes 1179648 | tf_op jit(solution)/shard_map/all_gather | solution.py:344
  12.2 17.7 %collective-permute-start = (bf16[320,1024]{1,0:T(8,128)(2,1)S(1)}, bf16[320,1024]{1,0:T(8,128)(2,1)S(1)}, u32[]{:S(2)}, u32[]{:S(2)}) collective-permute-start(bf16[320,1024]{1,0:T(8,128)(2,1)S(1)} %fusion.22), channel_id=1, source_target_pairs={{0,2},{1,3},{2,0},{3,1},{4,6},{5,7},{6,4},{7,5},{8,10},{9,11},{10,... | collective-permute-start | bytes 1966088 | tf_op jit(solution)/shard_map/ppermute | solution.py:259
  15.9 166.2 %all-gather.9.cloned.1.call-start = ((), (), s32[]{:S(2)}) async-start(), calls=%async_computation.2 | async-start | bytes 3244032 | tf_op jit(solution)/shard_map/all_gather | solution.py:344
  119.2 112.9 %all-gather.11.cloned.1.call-start = ((), (), s32[]{:S(2)}) async-start(), calls=%async_computation.3 | async-start | bytes 1179648 | tf_op jit(solution)/shard_map/all_gather | solution.py:344
  125.0 17.9 %collective-permute-start.3 = (bf16[320,1024]{1,0:T(8,128)(2,1)}, bf16[320,1024]{1,0:T(8,128)(2,1)}, u32[]{:S(2)}, u32[]{:S(2)}) collective-permute-start(bf16[320,1024]{1,0:T(8,128)(2,1)} %fusion.69), channel_id=1, source_target_pairs={{0,2},{1,3},{2,0},{3,1},{4,6},{5,7},{6,4},{7,5},{8,10},{9,11},{10,... | collective-permute-start | bytes 1966088 | tf_op jit(solution)/shard_map/ppermute | solution.py:259
  126.6 30.4 %collective-permute-start.8 = (bf16[320,1024]{1,0:T(8,128)(2,1)}, bf16[320,1024]{1,0:T(8,128)(2,1)}, u32[]{:S(2)}, u32[]{:S(2)}) collective-permute-start(bf16[320,1024]{1,0:T(8,128)(2,1)} %param.17), channel_id=1, source_target_pairs={{0,2},{1,3},{2,0},{3,1},{4,6},{5,7},{6,4},{7,5},{8,10},{9,11},{10,... | collective-permute-start | bytes 1966088 | tf_op jit(solution)/shard_map/ppermute | solution.py:259
  144.6 25.5 %collective-permute-start.4 = (bf16[320,1024]{1,0:T(8,128)(2,1)S(1)}, bf16[320,1024]{1,0:T(8,128)(2,1)S(1)}, u32[]{:S(2)}, u32[]{:S(2)}) collective-permute-start(bf16[320,1024]{1,0:T(8,128)(2,1)S(1)} %multiply_convert_fusion.4), channel_id=1, source_target_pairs={{0,2},{1,3},{2,0},{3,1},{4,6},{5,7},{6,4},{7,5},{8,10},{9,11},{10,... | collective-permute-start | bytes 1966088 | tf_op jit(solution)/shard_map/ppermute | solution.py:259
  158.5 14.3 %collective-permute-start.9 = (bf16[2,320,1024]{2,1,0:T(8,128)(2,1)S(1)}, bf16[2,320,1024]{2,1,0:T(8,128)(2,1)}, u32[]{:S(2)}, u32[]{:S(2)}) collective-permute-start(bf16[2,320,1024]{2,1,0:T(8,128)(2,1)S(1)} %pad_maximum_fusion.8), channel_id=1, source_target_pairs={{0,1},{1,0},{2,3},{3,2},{4,5},{5,4},{6,7},{7,6},{8,9},{9,8},{10,11... | collective-permute-start | bytes 3932168 | tf_op jit(solution)/shard_map/ppermute | solution.py:259
  307.4 72.6 %collective-permute-start.10 = (bf16[2,320,1024]{2,1,0:T(8,128)(2,1)}, bf16[2,320,1024]{2,1,0:T(8,128)(2,1)}, u32[]{:S(2)}, u32[]{:S(2)}) collective-permute-start(bf16[2,320,1024]{2,1,0:T(8,128)(2,1)} %fusion.35), channel_id=1, source_target_pairs={{0,1},{1,0},{2,3},{3,2},{4,5},{5,4},{6,7},{7,6},{8,9},{9,8},{10,11... | collective-permute-start | bytes 3932168 | tf_op jit(solution)/shard_map/ppermute | solution.py:259
  313.2 74.2 %collective-permute-start.6 = (bf16[2,320,1024]{2,1,0:T(8,128)(2,1)}, bf16[2,320,1024]{2,1,0:T(8,128)(2,1)}, u32[]{:S(2)}, u32[]{:S(2)}) collective-permute-start(bf16[2,320,1024]{2,1,0:T(8,128)(2,1)} %fusion.36), channel_id=1, source_target_pairs={{0,1},{1,0},{2,3},{3,2},{4,5},{5,4},{6,7},{7,6},{8,9},{9,8},{10,11... | collective-permute-start | bytes 3932168 | tf_op jit(solution)/shard_map/ppermute | solution.py:259
  323.1 20.9 %collective-permute-start.27 = (bf16[2,128,896]{2,1,0:T(8,128)(2,1)S(1)}, bf16[2,128,896]{2,1,0:T(8,128)(2,1)}, u32[]{:S(2)}, u32[]{:S(2)}) collective-permute-start(bf16[2,128,896]{2,1,0:T(8,128)(2,1)S(1)} %get-tuple-element.180), channel_id=1, source_target_pairs={{0,8},{4,12},{1,9},{5,13},{2,10},{6,14},{3,11},{7,15}} | collective-permute-start | bytes 1376264 | tf_op jit(solution)/shard_map/ppermute | solution.py:309
  326.6 31.7 %collective-permute-start.30 = (bf16[2,128,896]{2,1,0:T(8,128)(2,1)S(1)}, bf16[2,128,896]{2,1,0:T(8,128)(2,1)}, u32[]{:S(2)}, u32[]{:S(2)}) collective-permute-start(bf16[2,128,896]{2,1,0:T(8,128)(2,1)S(1)} %get-tuple-element.181), channel_id=1, source_target_pairs={{24,16},{28,20},{25,17},{29,21},{26,18},{30,22},{27,19},{31,23}} | collective-permute-start | bytes 1376264 | tf_op jit(solution)/shard_map/ppermute | solution.py:309
  344.0 13.5 %collective-permute-start.45 = (bf16[2,128,1024]{1,2,0:T(8,128)(2,1)S(1)}, bf16[2,128,1024]{1,2,0:T(8,128)(2,1)S(1)}, u32[]{:S(2)}, u32[]{:S(2)}) collective-permute-start(bf16[2,128,1024]{1,2,0:T(8,128)(2,1)S(1)} %bitcast.583), channel_id=1, source_target_pairs={{0,8},{4,12},{1,9},{5,13},{2,10},{6,14},{3,11},{7,15}} | collective-permute-start | bytes 1572872 | tf_op jit(solution)/shard_map/ppermute | solution.py:309
  346.5 20.9 %collective-permute-start.28 = (bf16[2,128,896]{2,1,0:T(8,128)(2,1)S(1)}, bf16[2,128,896]{2,1,0:T(8,128)(2,1)S(1)}, u32[]{:S(2)}, u32[]{:S(2)}) collective-permute-start(bf16[2,128,896]{2,1,0:T(8,128)(2,1)S(1)} %fusion.59), channel_id=1, source_target_pairs={{0,8},{4,12},{8,16},{12,20},{1,9},{5,13},{9,17},{13,21},{2,10},{6,... | collective-permute-start | bytes 1376264 | tf_op jit(solution)/shard_map/ppermute | solution.py:309
  357.5 11.8 %collective-permute-start.49 = (bf16[2,128,1024]{1,2,0:T(8,128)(2,1)S(1)}, bf16[2,128,1024]{1,2,0:T(8,128)(2,1)S(1)}, u32[]{:S(2)}, u32[]{:S(2)}) collective-permute-start(bf16[2,128,1024]{1,2,0:T(8,128)(2,1)S(1)} %fusion.47), channel_id=1, source_target_pairs={{24,16},{28,20},{16,8},{20,12},{25,17},{29,21},{17,9},{21,13},{26,... | collective-permute-start | bytes 1572872 | tf_op jit(solution)/shard_map/ppermute | solution.py:309
  358.3 20.2 %collective-permute-start.46 = (bf16[2,128,1024]{1,2,0:T(8,128)(2,1)S(1)}, bf16[2,128,1024]{1,2,0:T(8,128)(2,1)S(1)}, u32[]{:S(2)}, u32[]{:S(2)}) collective-permute-start(bf16[2,128,1024]{1,2,0:T(8,128)(2,1)S(1)} %fusion.49), channel_id=1, source_target_pairs={{0,8},{4,12},{8,16},{12,20},{1,9},{5,13},{9,17},{13,21},{2,10},{6,... | collective-permute-start | bytes 1572872 | tf_op jit(solution)/shard_map/ppermute | solution.py:309
  368.6 21.1 %collective-permute-start.31 = (bf16[2,128,896]{2,1,0:T(8,128)(2,1)S(1)}, bf16[2,128,896]{2,1,0:T(8,128)(2,1)S(1)}, u32[]{:S(2)}, u32[]{:S(2)}) collective-permute-start(bf16[2,128,896]{2,1,0:T(8,128)(2,1)S(1)} %get-tuple-element.179), channel_id=1, source_target_pairs={{24,16},{28,20},{16,8},{20,12},{25,17},{29,21},{17,9},{21,13},{26,... | collective-permute-start | bytes 1376264 | tf_op jit(solution)/shard_map/ppermute | solution.py:309
  369.3 57.7 %collective-permute-start.29 = (bf16[2,128,896]{2,1,0:T(8,128)(2,1)S(1)}, bf16[2,128,896]{2,1,0:T(8,128)(2,1)S(1)}, u32[]{:S(2)}, u32[]{:S(2)}) collective-permute-start(bf16[2,128,896]{2,1,0:T(8,128)(2,1)S(1)} %get-tuple-element.178), channel_id=1, source_target_pairs={{0,8},{4,12},{8,16},{12,20},{16,24},{20,28},{1,9},{5,13},{9,17},{1... | collective-permute-start | bytes 1376264 | tf_op jit(solution)/shard_map/ppermute | solution.py:309
  378.6 42.3 %collective-permute-start.50 = (bf16[2,128,1024]{1,2,0:T(8,128)(2,1)S(1)}, bf16[2,128,1024]{1,2,0:T(8,128)(2,1)S(1)}, u32[]{:S(2)}, u32[]{:S(2)}) collective-permute-start(bf16[2,128,1024]{1,2,0:T(8,128)(2,1)S(1)} %fusion.48), channel_id=1, source_target_pairs={{24,16},{28,20},{16,8},{20,12},{8,0},{12,4},{25,17},{29,21},{17,9}... | collective-permute-start | bytes 1572872 | tf_op jit(solution)/shard_map/ppermute | solution.py:309
  380.0 40.8 %collective-permute-start.47 = (bf16[2,128,1024]{1,2,0:T(8,128)(2,1)S(1)}, bf16[2,128,1024]{1,2,0:T(8,128)(2,1)S(1)}, u32[]{:S(2)}, u32[]{:S(2)}) collective-permute-start(bf16[2,128,1024]{1,2,0:T(8,128)(2,1)S(1)} %fusion.50), channel_id=1, source_target_pairs={{0,8},{4,12},{8,16},{12,20},{16,24},{20,28},{1,9},{5,13},{9,17},{1... | collective-permute-start | bytes 1572872 | tf_op jit(solution)/shard_map/ppermute | solution.py:309
  387.4 17.7 %collective-permute-start.11 = (bf16[320,1024]{1,0:T(8,128)(2,1)S(1)}, bf16[320,1024]{1,0:T(8,128)(2,1)S(1)}, u32[]{:S(2)}, u32[]{:S(2)}) collective-permute-start(bf16[320,1024]{1,0:T(8,128)(2,1)S(1)} %fusion.71), channel_id=1, source_target_pairs={{0,2},{1,3},{2,0},{3,1},{4,6},{5,7},{6,4},{7,5},{8,10},{9,11},{10,... | collective-permute-start | bytes 1966088 | tf_op jit(solution)/shard_map/ppermute | solution.py:259
  389.7 27.6 %collective-permute-start.7 = (bf16[320,1024]{1,0:T(8,128)(2,1)S(1)}, bf16[320,1024]{1,0:T(8,128)(2,1)S(1)}, u32[]{:S(2)}, u32[]{:S(2)}) collective-permute-start(bf16[320,1024]{1,0:T(8,128)(2,1)S(1)} %fusion.70), channel_id=1, source_target_pairs={{0,2},{1,3},{2,0},{3,1},{4,6},{5,7},{6,4},{7,5},{8,10},{9,11},{10,... | collective-permute-start | bytes 1966088 | tf_op jit(solution)/shard_map/ppermute | solution.py:259
  405.2 21.8 %collective-permute-start.32 = (bf16[2,128,896]{2,1,0:T(8,128)(2,1)S(1)}, bf16[2,128,896]{2,1,0:T(8,128)(2,1)S(1)}, u32[]{:S(2)}, u32[]{:S(2)}) collective-permute-start(bf16[2,128,896]{2,1,0:T(8,128)(2,1)S(1)} %fusion.58), channel_id=1, source_target_pairs={{24,16},{28,20},{16,8},{20,12},{8,0},{12,4},{25,17},{29,21},{17,9}... | collective-permute-start | bytes 1376264 | tf_op jit(solution)/shard_map/ppermute | solution.py:309
  420.5 14.8 %collective-permute-start.12 = (bf16[320,1024]{1,0:T(8,128)(2,1)S(1)}, bf16[320,1024]{1,0:T(8,128)(2,1)S(1)}, u32[]{:S(2)}, u32[]{:S(2)}) collective-permute-start(bf16[320,1024]{1,0:T(8,128)(2,1)S(1)} %get-tuple-element.136), channel_id=1, source_target_pairs={{0,2},{1,3},{2,0},{3,1},{4,6},{5,7},{6,4},{7,5},{8,10},{9,11},{10,... | collective-permute-start | bytes 1966088 | tf_op jit(solution)/shard_map/ppermute | solution.py:259
  421.1 14.6 %collective-permute-start.52 = (bf16[128,1024]{0,1:T(8,128)(2,1)S(1)}, bf16[128,1024]{0,1:T(8,128)(2,1)S(1)}, u32[]{:S(2)}, u32[]{:S(2)}) collective-permute-start(bf16[128,1024]{0,1:T(8,128)(2,1)S(1)} %get-tuple-element.218), channel_id=1, source_target_pairs={{4,0},{12,8},{20,16},{28,24},{5,1},{13,9},{21,17},{29,25},{6,2},{1... | collective-permute-start | bytes 786440 | tf_op jit(solution)/shard_map/ppermute | solution.py:309
  422.4 13.3 %collective-permute-start.51 = (bf16[128,1024]{0,1:T(8,128)(2,1)S(1)}, bf16[128,1024]{0,1:T(8,128)(2,1)S(1)}, u32[]{:S(2)}, u32[]{:S(2)}) collective-permute-start(bf16[128,1024]{0,1:T(8,128)(2,1)S(1)} %get-tuple-element.217), channel_id=1, source_target_pairs={{0,4},{8,12},{16,20},{24,28},{1,5},{9,13},{17,21},{25,29},{2,6},{1... | collective-permute-start | bytes 786440 | tf_op jit(solution)/shard_map/ppermute | solution.py:309
  427.2 9.4 %collective-permute-start.34 = (bf16[128,896]{1,0:T(8,128)(2,1)S(1)}, bf16[128,896]{1,0:T(8,128)(2,1)S(1)}, u32[]{:S(2)}, u32[]{:S(2)}) collective-permute-start(bf16[128,896]{1,0:T(8,128)(2,1)S(1)} %get-tuple-element.222), channel_id=1, source_target_pairs={{4,0},{12,8},{20,16},{28,24},{5,1},{13,9},{21,17},{29,25},{6,2},{1... | collective-permute-start | bytes 688136 | tf_op jit(solution)/shard_map/ppermute | solution.py:309
  428.5 8.1 %collective-permute-start.33 = (bf16[128,896]{1,0:T(8,128)(2,1)S(1)}, bf16[128,896]{1,0:T(8,128)(2,1)S(1)}, u32[]{:S(2)}, u32[]{:S(2)}) collective-permute-start(bf16[128,896]{1,0:T(8,128)(2,1)S(1)} %get-tuple-element.221), channel_id=1, source_target_pairs={{0,4},{8,12},{16,20},{24,28},{1,5},{9,13},{17,21},{25,29},{2,6},{1... | collective-permute-start | bytes 688136 | tf_op jit(solution)/shard_map/ppermute | solution.py:309
  514.8 71.0 %collective-permute-start.14 = (bf16[2,320,1024]{2,1,0:T(8,128)(2,1)}, bf16[2,320,1024]{2,1,0:T(8,128)(2,1)}, u32[]{:S(2)}, u32[]{:S(2)}) collective-permute-start(bf16[2,320,1024]{2,1,0:T(8,128)(2,1)} %fusion.37), channel_id=1, source_target_pairs={{0,1},{1,0},{2,3},{3,2},{4,5},{5,4},{6,7},{7,6},{8,9},{9,8},{10,11... | collective-permute-start | bytes 3932168 | tf_op jit(solution)/shard_map/ppermute | solution.py:259
  522.1 29.0 %collective-permute-start.19 = (bf16[2,128,896]{2,1,0:T(8,128)(2,1)}, bf16[2,128,896]{2,1,0:T(8,128)(2,1)}, u32[]{:S(2)}, u32[]{:S(2)}) collective-permute-start(bf16[2,128,896]{2,1,0:T(8,128)(2,1)} %get-tuple-element.176), channel_id=1, source_target_pairs={{0,8},{4,12},{1,9},{5,13},{2,10},{6,14},{3,11},{7,15}} | collective-permute-start | bytes 1376264 | tf_op jit(solution)/shard_map/ppermute | solution.py:309
  526.3 38.6 %collective-permute-start.22 = (bf16[2,128,896]{2,1,0:T(8,128)(2,1)S(1)}, bf16[2,128,896]{2,1,0:T(8,128)(2,1)}, u32[]{:S(2)}, u32[]{:S(2)}) collective-permute-start(bf16[2,128,896]{2,1,0:T(8,128)(2,1)S(1)} %get-tuple-element.177), channel_id=1, source_target_pairs={{24,16},{28,20},{25,17},{29,21},{26,18},{30,22},{27,19},{31,23}} | collective-permute-start | bytes 1376264 | tf_op jit(solution)/shard_map/ppermute | solution.py:309
  541.0 12.5 %collective-permute-start.40 = (bf16[2,128,1024]{1,2,0:T(8,128)(2,1)S(1)}, bf16[2,128,1024]{1,2,0:T(8,128)(2,1)S(1)}, u32[]{:S(2)}, u32[]{:S(2)}) collective-permute-start(bf16[2,128,1024]{1,2,0:T(8,128)(2,1)S(1)} %bitcast.580), channel_id=1, source_target_pairs={{24,16},{28,20},{25,17},{29,21},{26,18},{30,22},{27,19},{31,23}} | collective-permute-start | bytes 1572872 | tf_op jit(solution)/shard_map/ppermute | solution.py:309
  546.2 13.9 %collective-permute-start.37 = (bf16[2,128,1024]{1,2,0:T(8,128)(2,1)S(1)}, bf16[2,128,1024]{1,2,0:T(8,128)(2,1)S(1)}, u32[]{:S(2)}, u32[]{:S(2)}) collective-permute-start(bf16[2,128,1024]{1,2,0:T(8,128)(2,1)S(1)} %bitcast.582), channel_id=1, source_target_pairs={{0,8},{4,12},{1,9},{5,13},{2,10},{6,14},{3,11},{7,15}} | collective-permute-start | bytes 1572872 | tf_op jit(solution)/shard_map/ppermute | solution.py:309
  552.2 17.7 %collective-permute-start.20 = (bf16[2,128,896]{2,1,0:T(8,128)(2,1)S(1)}, bf16[2,128,896]{2,1,0:T(8,128)(2,1)S(1)}, u32[]{:S(2)}, u32[]{:S(2)}) collective-permute-start(bf16[2,128,896]{2,1,0:T(8,128)(2,1)S(1)} %fusion.64), channel_id=1, source_target_pairs={{0,8},{4,12},{8,16},{12,20},{1,9},{5,13},{9,17},{13,21},{2,10},{6,... | collective-permute-start | bytes 1376264 | tf_op jit(solution)/shard_map/ppermute | solution.py:309
  553.7 23.2 %collective-permute-start.41 = (bf16[2,128,1024]{1,2,0:T(8,128)(2,1)S(1)}, bf16[2,128,1024]{1,2,0:T(8,128)(2,1)S(1)}, u32[]{:S(2)}, u32[]{:S(2)}) collective-permute-start(bf16[2,128,1024]{1,2,0:T(8,128)(2,1)S(1)} %fusion.52), channel_id=1, source_target_pairs={{24,16},{28,20},{16,8},{20,12},{25,17},{29,21},{17,9},{21,13},{26,... | collective-permute-start | bytes 1572872 | tf_op jit(solution)/shard_map/ppermute | solution.py:309
  560.2 20.9 %collective-permute-start.38 = (bf16[2,128,1024]{1,2,0:T(8,128)(2,1)S(1)}, bf16[2,128,1024]{1,2,0:T(8,128)(2,1)S(1)}, u32[]{:S(2)}, u32[]{:S(2)}) collective-permute-start(bf16[2,128,1024]{1,2,0:T(8,128)(2,1)S(1)} %fusion.54), channel_id=1, source_target_pairs={{0,8},{4,12},{8,16},{12,20},{1,9},{5,13},{9,17},{13,21},{2,10},{6,... | collective-permute-start | bytes 1572872 | tf_op jit(solution)/shard_map/ppermute | solution.py:309
  571.2 16.3 %collective-permute-start.23 = (bf16[2,128,896]{2,1,0:T(8,128)(2,1)S(1)}, bf16[2,128,896]{2,1,0:T(8,128)(2,1)S(1)}, u32[]{:S(2)}, u32[]{:S(2)}) collective-permute-start(bf16[2,128,896]{2,1,0:T(8,128)(2,1)S(1)} %get-tuple-element.175), channel_id=1, source_target_pairs={{24,16},{28,20},{16,8},{20,12},{25,17},{29,21},{17,9},{21,13},{26,... | collective-permute-start | bytes 1376264 | tf_op jit(solution)/shard_map/ppermute | solution.py:309
  571.9 35.5 %collective-permute-start.21 = (bf16[2,128,896]{2,1,0:T(8,128)(2,1)S(1)}, bf16[2,128,896]{2,1,0:T(8,128)(2,1)S(1)}, u32[]{:S(2)}, u32[]{:S(2)}) collective-permute-start(bf16[2,128,896]{2,1,0:T(8,128)(2,1)S(1)} %get-tuple-element.174), channel_id=1, source_target_pairs={{0,8},{4,12},{8,16},{12,20},{16,24},{20,28},{1,9},{5,13},{9,17},{1... | collective-permute-start | bytes 1376264 | tf_op jit(solution)/shard_map/ppermute | solution.py:309
  577.0 15.0 %collective-permute-start.42 = (bf16[2,128,1024]{1,2,0:T(8,128)(2,1)S(1)}, bf16[2,128,1024]{1,2,0:T(8,128)(2,1)S(1)}, u32[]{:S(2)}, u32[]{:S(2)}) collective-permute-start(bf16[2,128,1024]{1,2,0:T(8,128)(2,1)S(1)} %fusion.53), channel_id=1, source_target_pairs={{24,16},{28,20},{16,8},{20,12},{8,0},{12,4},{25,17},{29,21},{17,9}... | collective-permute-start | bytes 1572872 | tf_op jit(solution)/shard_map/ppermute | solution.py:309
  581.3 19.8 %collective-permute-start.39 = (bf16[2,128,1024]{1,2,0:T(8,128)(2,1)S(1)}, bf16[2,128,1024]{1,2,0:T(8,128)(2,1)S(1)}, u32[]{:S(2)}, u32[]{:S(2)}) collective-permute-start(bf16[2,128,1024]{1,2,0:T(8,128)(2,1)S(1)} %fusion.55), channel_id=1, source_target_pairs={{0,8},{4,12},{8,16},{12,20},{16,24},{20,28},{1,9},{5,13},{9,17},{1... | collective-permute-start | bytes 1572872 | tf_op jit(solution)/shard_map/ppermute | solution.py:309
  587.6 19.7 %collective-permute-start.24 = (bf16[2,128,896]{2,1,0:T(8,128)(2,1)S(1)}, bf16[2,128,896]{2,1,0:T(8,128)(2,1)S(1)}, u32[]{:S(2)}, u32[]{:S(2)}) collective-permute-start(bf16[2,128,896]{2,1,0:T(8,128)(2,1)S(1)} %fusion.63), channel_id=1, source_target_pairs={{24,16},{28,20},{16,8},{20,12},{8,0},{12,4},{25,17},{29,21},{17,9}... | collective-permute-start | bytes 1376264 | tf_op jit(solution)/shard_map/ppermute | solution.py:309
  589.9 31.3 %collective-permute-start.15 = (bf16[320,1024]{1,0:T(8,128)(2,1)}, bf16[320,1024]{1,0:T(8,128)(2,1)}, u32[]{:S(2)}, u32[]{:S(2)}) collective-permute-start(bf16[320,1024]{1,0:T(8,128)(2,1)} %fusion.72), channel_id=1, source_target_pairs={{0,2},{1,3},{2,0},{3,1},{4,6},{5,7},{6,4},{7,5},{8,10},{9,11},{10,... | collective-permute-start | bytes 1966088 | tf_op jit(solution)/shard_map/ppermute | solution.py:259
  601.3 14.4 %collective-permute-start.44 = (bf16[128,1024]{0,1:T(8,128)(2,1)S(1)}, bf16[128,1024]{0,1:T(8,128)(2,1)S(1)}, u32[]{:S(2)}, u32[]{:S(2)}) collective-permute-start(bf16[128,1024]{0,1:T(8,128)(2,1)S(1)} %get-tuple-element.216), channel_id=1, source_target_pairs={{4,0},{12,8},{20,16},{28,24},{5,1},{13,9},{21,17},{29,25},{6,2},{1... | collective-permute-start | bytes 786440 | tf_op jit(solution)/shard_map/ppermute | solution.py:309
  602.6 13.1 %collective-permute-start.43 = (bf16[128,1024]{0,1:T(8,128)(2,1)S(1)}, bf16[128,1024]{0,1:T(8,128)(2,1)S(1)}, u32[]{:S(2)}, u32[]{:S(2)}) collective-permute-start(bf16[128,1024]{0,1:T(8,128)(2,1)S(1)} %get-tuple-element.215), channel_id=1, source_target_pairs={{0,4},{8,12},{16,20},{24,28},{1,5},{9,13},{17,21},{25,29},{2,6},{1... | collective-permute-start | bytes 786440 | tf_op jit(solution)/shard_map/ppermute | solution.py:309
  608.4 25.3 %collective-permute-start.26 = (bf16[128,896]{1,0:T(8,128)(2,1)}, bf16[128,896]{1,0:T(8,128)(2,1)}, u32[]{:S(2)}, u32[]{:S(2)}) collective-permute-start(bf16[128,896]{1,0:T(8,128)(2,1)} %get-tuple-element.220), channel_id=1, source_target_pairs={{4,0},{12,8},{20,16},{28,24},{5,1},{13,9},{21,17},{29,25},{6,2},{1... | collective-permute-start | bytes 688136 | tf_op jit(solution)/shard_map/ppermute | solution.py:309
  609.7 23.9 %collective-permute-start.25 = (bf16[128,896]{1,0:T(8,128)(2,1)}, bf16[128,896]{1,0:T(8,128)(2,1)}, u32[]{:S(2)}, u32[]{:S(2)}) collective-permute-start(bf16[128,896]{1,0:T(8,128)(2,1)} %get-tuple-element.219), channel_id=1, source_target_pairs={{0,4},{8,12},{16,20},{24,28},{1,5},{9,13},{17,21},{25,29},{2,6},{1... | collective-permute-start | bytes 688136 | tf_op jit(solution)/shard_map/ppermute | solution.py:309
  640.8 9.2 %collective-permute-start.36 = (f32[70144]{0:T(1024)S(1)}, f32[70144]{0:T(1024)S(1)}, u32[]{:S(2)}, u32[]{:S(2)}) collective-permute-start(f32[70144]{0:T(1024)S(1)} %fusion.145), channel_id=1, source_target_pairs={{0,2},{1,3},{2,0},{3,1},{4,6},{5,7},{6,4},{7,5},{8,10},{9,11},{10,... | collective-permute-start | bytes 841736 | tf_op jit(solution)/shard_map/ppermute | solution.py:290
  (174 other events, 1715.3 us)
Sparse Core Ops, SparseCore 0:
  11.7 60.3 all-gather.4
  74.7 38.1 all-gather.6
  119.3 56.6 all-gather.8
  178.5 38.7 all-gather.10

commit v2 on v1

--- a/solution.py
+++ b/solution.py
@@ -292,6 +292,19 @@
     return value
 
 
+def sum_parts(own, shared):
+    sums = sum_all(jnp.concatenate([value.reshape(-1) for value in own + shared]), "dp")
+    kept = sum(value.size for value in own)
+    across = sum_all(sums[kept:], "mp")
+    pieces = []
+    for group, flat in ((own, sums), (shared, across)):
+        place = 0
+        for value in group:
+            pieces.append(flat[place : place + value.size].reshape(value.shape))
+            place += value.size
+    return pieces
+
+
 def reduce_line(parts, place, size, device):
     own = lax.dynamic_index_in_dim(parts, place, 0, False)
     for way in (1, -1):
@@ -373,7 +386,8 @@
 
     result = current
     gradient = cotangent.astype(F32)
-    list_proj, list_own, list_shared = ([], [], [])
+    list_early, list_late, list_own, list_shared = ([], [], [], [])
+    late = None
     for depth in reversed(range(layers)):
         current, scale, gathered, raw, dt_in, x_act, bc_act, steps, rate, logs, skip, mixed_y, states, ratio, mixed = saved[depth]
         w_in, w_down = packed[depth]
@@ -392,7 +406,9 @@
         d_y = d_gated * gate_act
         d_z = d_gated * mixed_y * sigmoid_z * (1.0 + z_val * (1.0 - sigmoid_z))
         z_low = d_z.astype(BF16)
-        early = scatter_dp(jnp.concatenate([contract(gathered, z_low, TN), contract(grad_rows, mixed, TN)], axis=1))
+        early = jnp.concatenate([contract(gathered, z_low, TN), contract(grad_rows, mixed, TN)], axis=1)
+        d_y, early = lax.optimization_barrier((d_y, early))
+        early = scatter_dp(early)
         d_x, d_keys, d_reads, d_logs, d_steps, columns, x_dy = run_backward(x_act, bc_act, steps, logs, skip, states, d_y)
         columns = jnp.swapaxes(columns, 1, 2).reshape(steps.shape)
         d_ramps = block_sums(d_logs - steps * columns, True)
@@ -407,9 +423,13 @@
         d_low = jnp.concatenate(
             [d_xr.astype(BF16), d_bcr.astype(BF16), jnp.pad(d_dtr.astype(BF16), pad_heads)], axis=1
         )
+        if late is None:
+            d_low, early = lax.optimization_barrier((d_low, early))
+        else:
+            d_low, early, late = lax.optimization_barrier((d_low, early, late))
+            list_late.append(late)
         d_normed = scatter_mp(contract(z_low, w_in[:, :width], NT) + contract(d_low, w_in[:, width:], NT))
-        late = scatter_dp(contract(gathered, d_low, TN))
-        list_proj.append((early[:, :width], late[:, :width], late[:, width : width + pair], late[:, width + pair : width + pair + heads], early[:, width:].T))
+        list_early.append(early)
         gained = d_normed * in_gain[depth]
         g_gain_in = jnp.sum(d_normed * current * scale, axis=0)
         gradient = (
@@ -417,31 +437,33 @@
             + scale * gained
             - current * scale * scale * scale * jnp.mean(gained * current, axis=-1, keepdims=True)
         )
-        list_own.append((g_cxw, g_cxb, g_dtb, g_alog, g_skip, g_gain_norm))
-        list_shared.append((g_cbw, g_cbb, g_gain_in))
+        if depth > 0:
+            gradient, d_low = lax.optimization_barrier((gradient, d_low))
+        late = scatter_dp(contract(gathered, d_low, TN))
+        list_own.append(sum_parts([g_cxw, g_cxb, g_dtb, g_alog, g_skip, g_gain_norm], [g_cbw, g_cbb]))
+        list_shared.append(sum_all(sum_all(g_gain_in, "dp"), "mp"))
+    list_late.append(late)
+    list_proj = [
+        (
+            early[:, :width],
+            late[:, :width],
+            sum_all(late[:, width : width + pair], "mp"),
+            late[:, width + pair : width + pair + heads],
+            early[:, width:].T,
+        )
+        for early, late in zip(list_early, list_late)
+    ]
     proj = [jnp.stack([entry[i] for entry in list_proj[::-1]]) for i in range(5)]
-    own = [jnp.stack([entry[i] for entry in list_own[::-1]]) for i in range(6)]
-    shared = [jnp.stack([entry[i] for entry in list_shared[::-1]]) for i in range(3)]
-    sums = sum_all(jnp.concatenate([value.reshape(-1) for value in own + shared]), "dp")
-    kept = sum(value.size for value in own)
-    pieces, place = [], 0
-    for value in own:
-        pieces.append(sums[place : place + value.size].reshape(value.shape))
-        place += value.size
-    g_bc = proj[2]
-    across = sum_all(jnp.concatenate([sums[kept:], g_bc.reshape(-1)]), "mp")
-    place = 0
-    for value in shared + [g_bc]:
-        pieces.append(across[place : place + value.size].reshape(value.shape))
-        place += value.size
-    g_cxw, g_cxb, g_dtb, g_alog, g_skip, g_gain_norm, g_cbw, g_cbb, g_gain_in, g_bc = pieces
+    own = [jnp.stack([entry[i] for entry in list_own[::-1]]) for i in range(8)]
+    g_cxw, g_cxb, g_dtb, g_alog, g_skip, g_gain_norm, g_cbw, g_cbb = own
+    g_gain_in = jnp.stack(list_shared[::-1])
     return (
         result,
         gradient,
         g_gain_in,
         proj[0],
         proj[1],
-        g_bc,
+        proj[2],
         proj[3],
         g_cxw,
         g_cxb,

time: 670 us -> 721 us (1.076)
  other arithmetic: 111 us -> 149 us
  waiting for transfers between devices: 166 us -> 202 us
  local copies, waits for them, and re-layouts: 122 us -> 93.6 us
  starting transfers between devices: 99.4 us -> 109 us
    ppermute x32, waiting for transfers between devices: 37.7 us -> 68.9 us  [reduce_line(): sent = lax.ppermute(part.astype(BF16), 'dp', pairs)]
    unnamed x348 -> x345, local copies, waits for them, and re-layouts: 49.1 us -> 28.1 us
    ppermute x5 -> x24, starting transfers between devices: 4.45 us -> 21 us  [sum_all(): lax.ppermute(value, axis, [(i, i ^ bit) for i in range(size)])]
    convert_element_type x14, other arithmetic: 5.92 us -> 20.7 us  [reduce_line(): sent = lax.ppermute(part.astype(BF16), 'dp', pairs)]
    mul x4, other arithmetic: 4.04 us -> 13.3 us  [causal_conv(): summed = summed + padded[:, tap:tap + LEN, :] * kernel[tap]]
    ppermute x5 -> x24, waiting for transfers between devices: 11.7 us -> 19.4 us  [sum_all(): lax.ppermute(value, axis, [(i, i ^ bit) for i in range(size)])]
    ppermute x32, starting transfers between devices: 83.2 us -> 75.6 us  [reduce_line(): sent = lax.ppermute(part.astype(BF16), 'dp', pairs)]
  transfers between devices with their start and end apart: 57 -> 76, of which waited for: 22 -> 41; matrix products, arithmetic and copies ran while one was open for 25% -> 32% of each run, Pallas kernels for 2% -> 8%
where the time goes in v2:
time: 721 us; the launch traced here: 710 us
  waiting for transfers between devices  202 us (28%)
  other arithmetic  149 us (21%)
  starting transfers between devices  109 us (15%)
  local copies, waits for them, and re-layouts  93.6 us (13%)
  Pallas kernels  57 us (8%)
  matrix products  56.8 us (8%)
  blocking collectives  25.7 us (4%)
  between operations  17 us (2%)
    ppermute x32, starting transfers between devices, reduce_line(): sent = lax.ppermute(part.astype(BF16), 'dp', pairs)  75.6 us
    ppermute x16, waiting for transfers between devices, swap_mp(): return lax.ppermute(value, 'mp', [(i, i ^ bit) for i in range(size)])  75.5 us
    ppermute x32, waiting for transfers between devices, reduce_line(): sent = lax.ppermute(part.astype(BF16), 'dp', pairs)  68.9 us
    dot_general x16, matrix products, contract(): lax.dot_general(left, right, (dims, ((), ())), preferred_element_type=F32)  55 us
    pallas_call x2, Pallas kernels, run_backward(): pl.pallas_call(functools.partial(scan_backward, heads), grid=grid, in_spe...  44.1 us
    all_gather x4, waiting for transfers between devices, body(): lax.all_gather(part, 'dp', axis=0, tiled=True)  38.1 us
    unnamed x345, local copies, waits for them, and re-layouts  28.1 us
    ppermute x24, starting transfers between devices, sum_all(): lax.ppermute(value, axis, [(i, i ^ bit) for i in range(size)])  21 us
  transfers between devices with their start and end apart: 76, of which 41 were waited for; matrix products, arithmetic and copies ran while one was open for 32% of the time, Pallas kernels for 8%

profile of v2, /device:TPU:0, one launch (start us, length us, event | category | flops | bytes accessed | tf_op | source)
XLA Modules:
  0.0 710.0 jit_solution(6471727431528959582)
XLA Ops:
  17.4 12.5 %collective-permute-done = bf16[320,1024]{1,0:T(8,128)(2,1)S(1)} collective-permute-done((bf16[320,1024]{1,0:T(8,128)(2,1)S(1)}, bf16[320,1024]{1,0:T(8,128)(2,1)S(1)}, u32[]{:S(2)}, u32[]{:S(2)}) %collective-permute-start) | collective-permute-done | bytes 655392 | tf_op jit(solution)/shard_map/ppermute | solution.py:259
  36.0 36.1 %all-gather.5.cloned.1.call-done = bf16[1024,1408]{1,0:T(8,128)(2,1)} async-done(((bf16[128,1408]{1,0:T(8,128)(2,1)}), bf16[1024,1408]{1,0:T(8,128)(2,1)}) %all-gather.5.cloned.1.call-update) | async-done | bytes 2883600 | tf_op jit(solution)/shard_map/all_gather | solution.py:357
  72.1 6.9 fusion.149
  85.0 6.2 multiply_bitcast_fusion.1
  95.5 6.5 scan_forward.2
  103.9 6.4 psum.28
  126.1 15.9 %collective-permute-done.3 = bf16[320,1024]{1,0:T(8,128)(2,1)} collective-permute-done((bf16[320,1024]{1,0:T(8,128)(2,1)}, bf16[320,1024]{1,0:T(8,128)(2,1)}, u32[]{:S(2)}, u32[]{:S(2)}) %collective-permute-start.3) | collective-permute-done | bytes 655392 | tf_op jit(solution)/shard_map/ppermute | solution.py:259
  145.2 10.8 %collective-permute-done.8 = bf16[320,1024]{1,0:T(8,128)(2,1)} collective-permute-done((bf16[320,1024]{1,0:T(8,128)(2,1)}, bf16[320,1024]{1,0:T(8,128)(2,1)}, u32[]{:S(2)}, u32[]{:S(2)}) %collective-permute-start.8) | collective-permute-done | bytes 655392 | tf_op jit(solution)/shard_map/ppermute | solution.py:259
  158.6 10.5 %collective-permute-done.4 = bf16[320,1024]{1,0:T(8,128)(2,1)S(1)} collective-permute-done((bf16[320,1024]{1,0:T(8,128)(2,1)S(1)}, bf16[320,1024]{1,0:T(8,128)(2,1)S(1)}, u32[]{:S(2)}, u32[]{:S(2)}) %collective-permute-start.4) | collective-permute-done | bytes 655392 | tf_op jit(solution)/shard_map/ppermute | solution.py:259
  176.5 7.0 fusion.150
  187.3 5.4 multiply_bitcast_fusion.2
  192.7 4.5 multiply_bitcast_fusion
  203.1 6.4 scan_forward.3
  209.6 4.4 multiply_reduce_fusion.12
  214.0 7.6 %psum.29 = f32[1280]{0:T(1024)S(1)} all-reduce(f32[1280]{0:T(1024)S(1)} %get-tuple-element.158), channel_id=1, replica_groups=mesh['dp'=8,'mp'=4] {'mp'}, use_global_device_ids=true, to_apply=%region_5.6 | all-reduce | flops 1280 | bytes 10240 | tf_op jit(solution)/shard_map/psum | solution.py:380
  221.6 5.5 fusion.131
  227.1 6.8 multiply_reduce_fusion
  233.9 6.0 psum.30
  239.9 5.4 multiply_convert_fusion.1
  250.6 6.6 reshape.418
  267.1 21.9 %scan_backward.2 = (f32[1280,512]{1,0:T(8,128)S(1)}, f32[1280,128]{1,0:T(8,128)S(1)}, f32[1280,128]{1,0:T(8,128)S(1)}, f32[1280,8]{1,0:T(8,128)S(1)}, f32[1280,8...) custom-call(f32[1280,512]{1,0:T(8,128)S(1)} %copy-done.5, f32[1280,256]{1,0:T(8,128)S(1)} %copy-done.9, ...), custom_call_target="tpu_custom_call" | custom-call | flops 16106127360 | bytes 13107200 | tf_op jit(solution)/shard_map/scan_backward/pallas_call | solution.py:225
  289.0 4.1 multiply_reduce_fusion.3
  293.2 4.4 broadcast_multiply_fusion.1
  303.2 4.4 constant_dynamic-slice_fusion.11
  323.7 4.4 collective-permute-start.12
  338.4 5.8 collective-permute-done.15
  352.0 4.7 collective-permute-done.17
  371.7 4.6 copy.153
  376.3 9.0 %collective-permute-done.19 = bf16[320,1024]{1,0:T(8,128)(2,1)S(1)} collective-permute-done((bf16[320,1024]{1,0:T(8,128)(2,1)}, bf16[320,1024]{1,0:T(8,128)(2,1)S(1)}, u32[]{:S(2)}, u32[]{:S(2)}) %collective-permute-start.19) | collective-permute-done | bytes 655392 | tf_op jit(solution)/shard_map/ppermute | solution.py:259
  387.1 11.9 %collective-permute-done.7 = bf16[320,1024]{1,0:T(8,128)(2,1)S(1)} collective-permute-done((bf16[320,1024]{1,0:T(8,128)(2,1)}, bf16[320,1024]{1,0:T(8,128)(2,1)S(1)}, u32[]{:S(2)}, u32[]{:S(2)}) %collective-permute-start.7) | collective-permute-done | bytes 655392 | tf_op jit(solution)/shard_map/ppermute | solution.py:259
  408.0 8.9 %collective-permute-done.30 = bf16[2,128,896]{2,1,0:T(8,128)(2,1)S(1)} collective-permute-done((bf16[2,128,896]{2,1,0:T(8,128)(2,1)S(1)}, bf16[2,128,896]{2,1,0:T(8,128)(2,1)S(1)}, u32[]{:S(2)}, u32[]{:S(2)}) %collective-permute-start.30) | collective-permute-done | bytes 458784 | tf_op jit(solution)/shard_map/ppermute | solution.py:322
  417.0 4.4 collective-permute-start.31
  422.7 7.4 %collective-permute-done.31 = bf16[2,128,896]{2,1,0:T(8,128)(2,1)S(1)} collective-permute-done((bf16[2,128,896]{2,1,0:T(8,128)(2,1)S(1)}, bf16[2,128,896]{2,1,0:T(8,128)(2,1)S(1)}, u32[]{:S(2)}, u32[]{:S(2)}) %collective-permute-start.31) | collective-permute-done | bytes 458784 | tf_op jit(solution)/shard_map/ppermute | solution.py:322
  459.4 6.2 collective-permute-done.35
  480.8 5.7 psum.31
  486.6 5.4 multiply_convert_fusion
  497.2 6.6 reshape.426
  503.8 5.4 constant_dynamic-slice_fusion.4
  518.9 22.2 %scan_backward.3 = (f32[1280,512]{1,0:T(8,128)S(1)}, f32[1280,128]{1,0:T(8,128)S(1)}, f32[1280,128]{1,0:T(8,128)S(1)}, f32[1280,8]{1,0:T(8,128)S(1)}, f32[1280,8...) custom-call(f32[1280,512]{1,0:T(8,128)S(1)} %copy-done.3, f32[1280,256]{1,0:T(8,128)S(1)} %copy-done.7, ...), custom_call_target="tpu_custom_call" | custom-call | flops 16106127360 | bytes 13107200 | tf_op jit(solution)/shard_map/scan_backward/pallas_call | solution.py:225
  544.8 4.5 broadcast_multiply_fusion
  556.0 5.6 fusion.39
  576.6 4.9 collective-permute-start.23
  587.1 5.3 collective-permute-done.23
  594.3 4.4 collective-permute-start.24
  609.6 6.1 collective-permute-done.27
  622.1 4.4 collective-permute-done.29
  644.8 6.9 collective-permute-done.51
  664.5 4.3 collective-permute-start.52
  (703 shorter events, 321.8 us)
Async XLA Ops:
  7.2 64.9 %all-gather.5.cloned.1.call-start = ((), (), s32[]{:S(2)}) async-start(), calls=%async_computation | async-start | bytes 3244032 | tf_op jit(solution)/shard_map/all_gather | solution.py:357
  11.6 101.3 %all-gather.7.cloned.1.call-start = ((), (), s32[]{:S(2)}) async-start(), calls=%async_computation.1 | async-start | bytes 1179648 | tf_op jit(solution)/shard_map/all_gather | solution.py:357
  12.2 17.7 %collective-permute-start = (bf16[320,1024]{1,0:T(8,128)(2,1)S(1)}, bf16[320,1024]{1,0:T(8,128)(2,1)S(1)}, u32[]{:S(2)}, u32[]{:S(2)}) collective-permute-start(bf16[320,1024]{1,0:T(8,128)(2,1)S(1)} %fusion.22), channel_id=1, source_target_pairs={{0,2},{1,3},{2,0},{3,1},{4,6},{5,7},{6,4},{7,5},{8,10},{9,11},{10,... | collective-permute-start | bytes 1966088 | tf_op jit(solution)/shard_map/ppermute | solution.py:259
  15.9 160.6 %all-gather.9.cloned.1.call-start = ((), (), s32[]{:S(2)}) async-start(), calls=%async_computation.2 | async-start | bytes 3244032 | tf_op jit(solution)/shard_map/all_gather | solution.py:357
  119.3 107.8 %all-gather.11.cloned.1.call-start = ((), (), s32[]{:S(2)}) async-start(), calls=%async_computation.3 | async-start | bytes 1179648 | tf_op jit(solution)/shard_map/all_gather | solution.py:357
  124.1 17.9 %collective-permute-start.3 = (bf16[320,1024]{1,0:T(8,128)(2,1)}, bf16[320,1024]{1,0:T(8,128)(2,1)}, u32[]{:S(2)}, u32[]{:S(2)}) collective-permute-start(bf16[320,1024]{1,0:T(8,128)(2,1)} %fusion.69), channel_id=1, source_target_pairs={{0,2},{1,3},{2,0},{3,1},{4,6},{5,7},{6,4},{7,5},{8,10},{9,11},{10,... | collective-permute-start | bytes 1966088 | tf_op jit(solution)/shard_map/ppermute | solution.py:259
  125.6 30.4 %collective-permute-start.8 = (bf16[320,1024]{1,0:T(8,128)(2,1)}, bf16[320,1024]{1,0:T(8,128)(2,1)}, u32[]{:S(2)}, u32[]{:S(2)}) collective-permute-start(bf16[320,1024]{1,0:T(8,128)(2,1)} %param.17), channel_id=1, source_target_pairs={{0,2},{1,3},{2,0},{3,1},{4,6},{5,7},{6,4},{7,5},{8,10},{9,11},{10,... | collective-permute-start | bytes 1966088 | tf_op jit(solution)/shard_map/ppermute | solution.py:259
  143.6 25.5 %collective-permute-start.4 = (bf16[320,1024]{1,0:T(8,128)(2,1)S(1)}, bf16[320,1024]{1,0:T(8,128)(2,1)S(1)}, u32[]{:S(2)}, u32[]{:S(2)}) collective-permute-start(bf16[320,1024]{1,0:T(8,128)(2,1)S(1)} %multiply_convert_fusion.4), channel_id=1, source_target_pairs={{0,2},{1,3},{2,0},{3,1},{4,6},{5,7},{6,4},{7,5},{8,10},{9,11},{10,... | collective-permute-start | bytes 1966088 | tf_op jit(solution)/shard_map/ppermute | solution.py:259
  158.6 12.3 %collective-permute-start.9 = (bf16[2,320,1024]{2,1,0:T(8,128)(2,1)}, bf16[2,320,1024]{2,1,0:T(8,128)(2,1)}, u32[]{:S(2)}, u32[]{:S(2)}) collective-permute-start(bf16[2,320,1024]{2,1,0:T(8,128)(2,1)} %pad_maximum_fusion.8), channel_id=1, source_target_pairs={{0,1},{1,0},{2,3},{3,2},{4,5},{5,4},{6,7},{7,6},{8,9},{9,8},{10,11... | collective-permute-start | bytes 3932168 | tf_op jit(solution)/shard_map/ppermute | solution.py:259
  260.5 47.1 %collective-permute-start.10 = (bf16[2,128,1024]{1,2,0:T(8,128)(2,1)}, bf16[2,128,1024]{1,2,0:T(8,128)(2,1)}, u32[]{:S(2)}, u32[]{:S(2)}) collective-permute-start(bf16[2,128,1024]{1,2,0:T(8,128)(2,1)} %bitcast.524), channel_id=1, source_target_pairs={{0,8},{4,12},{1,9},{5,13},{2,10},{6,14},{3,11},{7,15}} | collective-permute-start | bytes 1572872 | tf_op jit(solution)/shard_map/ppermute | solution.py:322
  264.1 47.5 %collective-permute-start.13 = (bf16[2,128,1024]{1,2,0:T(8,128)(2,1)}, bf16[2,128,1024]{1,2,0:T(8,128)(2,1)}, u32[]{:S(2)}, u32[]{:S(2)}) collective-permute-start(bf16[2,128,1024]{1,2,0:T(8,128)(2,1)} %bitcast.525), channel_id=1, source_target_pairs={{24,16},{28,20},{25,17},{29,21},{26,18},{30,22},{27,19},{31,23}} | collective-permute-start | bytes 1572872 | tf_op jit(solution)/shard_map/ppermute | solution.py:322
  309.5 12.8 %collective-permute-start.11 = (bf16[2,128,1024]{1,2,0:T(8,128)(2,1)}, bf16[2,128,1024]{1,2,0:T(8,128)(2,1)}, u32[]{:S(2)}, u32[]{:S(2)}) collective-permute-start(bf16[2,128,1024]{1,2,0:T(8,128)(2,1)} %fusion.54), channel_id=1, source_target_pairs={{0,8},{4,12},{8,16},{12,20},{1,9},{5,13},{9,17},{13,21},{2,10},{6,... | collective-permute-start | bytes 1572872 | tf_op jit(solution)/shard_map/ppermute | solution.py:322
  313.5 14.6 %collective-permute-start.14 = (bf16[2,128,1024]{1,2,0:T(8,128)(2,1)}, bf16[2,128,1024]{1,2,0:T(8,128)(2,1)}, u32[]{:S(2)}, u32[]{:S(2)}) collective-permute-start(bf16[2,128,1024]{1,2,0:T(8,128)(2,1)} %fusion.52), channel_id=1, source_target_pairs={{24,16},{28,20},{16,8},{20,12},{25,17},{29,21},{17,9},{21,13},{26,... | collective-permute-start | bytes 1572872 | tf_op jit(solution)/shard_map/ppermute | solution.py:322
  323.7 14.7 %collective-permute-start.12 = (bf16[2,128,1024]{1,2,0:T(8,128)(2,1)S(1)}, bf16[2,128,1024]{1,2,0:T(8,128)(2,1)S(1)}, u32[]{:S(2)}, u32[]{:S(2)}) collective-permute-start(bf16[2,128,1024]{1,2,0:T(8,128)(2,1)S(1)} %fusion.55), channel_id=1, source_target_pairs={{0,8},{4,12},{8,16},{12,20},{16,24},{20,28},{1,9},{5,13},{9,17},{1... | collective-permute-start | bytes 1572872 | tf_op jit(solution)/shard_map/ppermute | solution.py:322
  329.8 14.4 %collective-permute-start.15 = (bf16[2,128,1024]{1,2,0:T(8,128)(2,1)S(1)}, bf16[2,128,1024]{1,2,0:T(8,128)(2,1)S(1)}, u32[]{:S(2)}, u32[]{:S(2)}) collective-permute-start(bf16[2,128,1024]{1,2,0:T(8,128)(2,1)S(1)} %fusion.53), channel_id=1, source_target_pairs={{24,16},{28,20},{16,8},{20,12},{8,0},{12,4},{25,17},{29,21},{17,9}... | collective-permute-start | bytes 1572872 | tf_op jit(solution)/shard_map/ppermute | solution.py:322
  348.2 8.5 %collective-permute-start.17 = (bf16[128,1024]{0,1:T(8,128)(2,1)S(1)}, bf16[128,1024]{0,1:T(8,128)(2,1)S(1)}, u32[]{:S(2)}, u32[]{:S(2)}) collective-permute-start(bf16[128,1024]{0,1:T(8,128)(2,1)S(1)} %get-tuple-element.239), channel_id=1, source_target_pairs={{4,0},{12,8},{20,16},{28,24},{5,1},{13,9},{21,17},{29,25},{6,2},{1... | collective-permute-start | bytes 786440 | tf_op jit(solution)/shard_map/ppermute | solution.py:322
  367.5 17.7 %collective-permute-start.19 = (bf16[320,1024]{1,0:T(8,128)(2,1)}, bf16[320,1024]{1,0:T(8,128)(2,1)S(1)}, u32[]{:S(2)}, u32[]{:S(2)}) collective-permute-start(bf16[320,1024]{1,0:T(8,128)(2,1)} %fusion.71), channel_id=1, source_target_pairs={{0,2},{1,3},{2,0},{3,1},{4,6},{5,7},{6,4},{7,5},{8,10},{9,11},{10,... | collective-permute-start | bytes 1966088 | tf_op jit(solution)/shard_map/ppermute | solution.py:259
  370.6 28.3 %collective-permute-start.7 = (bf16[320,1024]{1,0:T(8,128)(2,1)}, bf16[320,1024]{1,0:T(8,128)(2,1)S(1)}, u32[]{:S(2)}, u32[]{:S(2)}) collective-permute-start(bf16[320,1024]{1,0:T(8,128)(2,1)} %fusion.70), channel_id=1, source_target_pairs={{0,2},{1,3},{2,0},{3,1},{4,6},{5,7},{6,4},{7,5},{8,10},{9,11},{10,... | collective-permute-start | bytes 1966088 | tf_op jit(solution)/shard_map/ppermute | solution.py:259
  405.1 11.8 %collective-permute-start.30 = (bf16[2,128,896]{2,1,0:T(8,128)(2,1)S(1)}, bf16[2,128,896]{2,1,0:T(8,128)(2,1)S(1)}, u32[]{:S(2)}, u32[]{:S(2)}) collective-permute-start(bf16[2,128,896]{2,1,0:T(8,128)(2,1)S(1)} %get-tuple-element.200), channel_id=1, source_target_pairs={{0,8},{4,12},{1,9},{5,13},{2,10},{6,14},{3,11},{7,15}} | collective-permute-start | bytes 1376264 | tf_op jit(solution)/shard_map/ppermute | solution.py:322
  407.3 15.4 %collective-permute-start.33 = (bf16[2,128,896]{2,1,0:T(8,128)(2,1)S(1)}, bf16[2,128,896]{2,1,0:T(8,128)(2,1)S(1)}, u32[]{:S(2)}, u32[]{:S(2)}) collective-permute-start(bf16[2,128,896]{2,1,0:T(8,128)(2,1)S(1)} %get-tuple-element.201), channel_id=1, source_target_pairs={{24,16},{28,20},{25,17},{29,21},{26,18},{30,22},{27,19},{31,23}} | collective-permute-start | bytes 1376264 | tf_op jit(solution)/shard_map/ppermute | solution.py:322
  417.0 13.1 %collective-permute-start.31 = (bf16[2,128,896]{2,1,0:T(8,128)(2,1)S(1)}, bf16[2,128,896]{2,1,0:T(8,128)(2,1)S(1)}, u32[]{:S(2)}, u32[]{:S(2)}) collective-permute-start(bf16[2,128,896]{2,1,0:T(8,128)(2,1)S(1)} %fusion.64), channel_id=1, source_target_pairs={{0,8},{4,12},{8,16},{12,20},{1,9},{5,13},{9,17},{13,21},{2,10},{6,... | collective-permute-start | bytes 1376264 | tf_op jit(solution)/shard_map/ppermute | solution.py:322
  421.5 15.2 %collective-permute-start.20 = (bf16[320,1024]{1,0:T(8,128)(2,1)S(1)}, bf16[320,1024]{1,0:T(8,128)(2,1)S(1)}, u32[]{:S(2)}, u32[]{:S(2)}) collective-permute-start(bf16[320,1024]{1,0:T(8,128)(2,1)S(1)} %convert_element_type.428), channel_id=1, source_target_pairs={{0,2},{1,3},{2,0},{3,1},{4,6},{5,7},{6,4},{7,5},{8,10},{9,11},{10,... | collective-permute-start | bytes 1966088 | tf_op jit(solution)/shard_map/ppermute | solution.py:259
  431.2 18.8 %collective-permute-start.34 = (bf16[2,128,896]{2,1,0:T(8,128)(2,1)}, bf16[2,128,896]{2,1,0:T(8,128)(2,1)}, u32[]{:S(2)}, u32[]{:S(2)}) collective-permute-start(bf16[2,128,896]{2,1,0:T(8,128)(2,1)} %get-tuple-element.199), channel_id=1, source_target_pairs={{24,16},{28,20},{16,8},{20,12},{25,17},{29,21},{17,9},{21,13},{26,... | collective-permute-start | bytes 1376264 | tf_op jit(solution)/shard_map/ppermute | solution.py:322
  439.0 31.9 %collective-permute-start.21 = (bf16[2,320,1024]{2,1,0:T(8,128)(2,1)}, bf16[2,320,1024]{2,1,0:T(8,128)(2,1)}, u32[]{:S(2)}, u32[]{:S(2)}) collective-permute-start(bf16[2,320,1024]{2,1,0:T(8,128)(2,1)} %pad_maximum_fusion.9), channel_id=1, source_target_pairs={{0,1},{1,0},{2,3},{3,2},{4,5},{5,4},{6,7},{7,6},{8,9},{9,8},{10,11... | collective-permute-start | bytes 3932168 | tf_op jit(solution)/shard_map/ppermute | solution.py:259
  447.1 12.3 %collective-permute-start.32 = (bf16[2,128,896]{2,1,0:T(8,128)(2,1)}, bf16[2,128,896]{2,1,0:T(8,128)(2,1)S(1)}, u32[]{:S(2)}, u32[]{:S(2)}) collective-permute-start(bf16[2,128,896]{2,1,0:T(8,128)(2,1)} %get-tuple-element.198), channel_id=1, source_target_pairs={{0,8},{4,12},{8,16},{12,20},{16,24},{20,28},{1,9},{5,13},{9,17},{1... | collective-permute-start | bytes 1376264 | tf_op jit(solution)/shard_map/ppermute | solution.py:322
  452.2 13.4 %collective-permute-start.35 = (bf16[2,128,896]{2,1,0:T(8,128)(2,1)}, bf16[2,128,896]{2,1,0:T(8,128)(2,1)S(1)}, u32[]{:S(2)}, u32[]{:S(2)}) collective-permute-start(bf16[2,128,896]{2,1,0:T(8,128)(2,1)} %fusion.63), channel_id=1, source_target_pairs={{24,16},{28,20},{16,8},{20,12},{8,0},{12,4},{25,17},{29,21},{17,9}... | collective-permute-start | bytes 1376264 | tf_op jit(solution)/shard_map/ppermute | solution.py:322
  467.9 152.2 %collective-permute-start.36 = (bf16[128,896]{1,0:T(8,128)(2,1)}, bf16[128,896]{1,0:T(8,128)(2,1)}, u32[]{:S(2)}, u32[]{:S(2)}) collective-permute-start(bf16[128,896]{1,0:T(8,128)(2,1)} %get-tuple-element.242), channel_id=1, source_target_pairs={{0,4},{8,12},{16,20},{24,28},{1,5},{9,13},{17,21},{25,29},{2,6},{1... | collective-permute-start | bytes 688136 | tf_op jit(solution)/shard_map/ppermute | solution.py:322
  512.5 62.2 %collective-permute-start.22 = (bf16[2,128,1024]{1,2,0:T(8,128)(2,1)}, bf16[2,128,1024]{1,2,0:T(8,128)(2,1)}, u32[]{:S(2)}, u32[]{:S(2)}) collective-permute-start(bf16[2,128,1024]{1,2,0:T(8,128)(2,1)} %bitcast.526), channel_id=1, source_target_pairs={{0,8},{4,12},{1,9},{5,13},{2,10},{6,14},{3,11},{7,15}} | collective-permute-start | bytes 1572872 | tf_op jit(solution)/shard_map/ppermute | solution.py:322
  517.1 64.4 %collective-permute-start.25 = (bf16[2,128,1024]{1,2,0:T(8,128)(2,1)}, bf16[2,128,1024]{1,2,0:T(8,128)(2,1)}, u32[]{:S(2)}, u32[]{:S(2)}) collective-permute-start(bf16[2,128,1024]{1,2,0:T(8,128)(2,1)} %bitcast.527), channel_id=1, source_target_pairs={{24,16},{28,20},{25,17},{29,21},{26,18},{30,22},{27,19},{31,23}} | collective-permute-start | bytes 1572872 | tf_op jit(solution)/shard_map/ppermute | solution.py:322
  554.0 8.4 %collective-permute-start.65 = (f32[4376]{0:T(1024)S(1)}, f32[4376]{0:T(1024)S(1)}, u32[]{:S(2)}, u32[]{:S(2)}) collective-permute-start(f32[4376]{0:T(1024)S(1)} %concatenate.39), channel_id=1, source_target_pairs={{0,4},{4,0},{8,12},{12,8},{16,20},{20,16},{24,28},{28,24},{1,5},{5... | collective-permute-start | bytes 52520 | tf_op jit(solution)/shard_map/ppermute | solution.py:290
  573.0 29.1 %collective-permute-start.68 = (f32[1280]{0:T(1024)S(1)}, f32[1280]{0:T(1024)S(1)}, u32[]{:S(2)}, u32[]{:S(2)}) collective-permute-start(f32[1280]{0:T(1024)S(1)} %slice.485), channel_id=1, source_target_pairs={{0,1},{1,0},{2,3},{3,2},{4,5},{5,4},{6,7},{7,6},{8,9},{9,8},{10,11... | collective-permute-start | bytes 15368 | tf_op jit(solution)/shard_map/ppermute | solution.py:290
  573.0 30.4 %collective-permute-start.70 = (f32[1280]{0:T(1024)S(1)}, f32[1280]{0:T(1024)S(1)}, u32[]{:S(2)}, u32[]{:S(2)}) collective-permute-start(f32[1280]{0:T(1024)S(1)} %slice.487), channel_id=1, source_target_pairs={{0,1},{1,0},{2,3},{3,2},{4,5},{5,4},{6,7},{7,6},{8,9},{9,8},{10,11... | collective-permute-start | bytes 15368 | tf_op jit(solution)/shard_map/ppermute | solution.py:290
  576.6 15.8 %collective-permute-start.23 = (bf16[2,128,1024]{1,2,0:T(8,128)(2,1)}, bf16[2,128,1024]{1,2,0:T(8,128)(2,1)}, u32[]{:S(2)}, u32[]{:S(2)}) collective-permute-start(bf16[2,128,1024]{1,2,0:T(8,128)(2,1)} %fusion.49), channel_id=1, source_target_pairs={{0,8},{4,12},{8,16},{12,20},{1,9},{5,13},{9,17},{13,21},{2,10},{6,... | collective-permute-start | bytes 1572872 | tf_op jit(solution)/shard_map/ppermute | solution.py:322
  583.5 15.3 %collective-permute-start.26 = (bf16[2,128,1024]{1,2,0:T(8,128)(2,1)}, bf16[2,128,1024]{1,2,0:T(8,128)(2,1)}, u32[]{:S(2)}, u32[]{:S(2)}) collective-permute-start(bf16[2,128,1024]{1,2,0:T(8,128)(2,1)} %fusion.47), channel_id=1, source_target_pairs={{24,16},{28,20},{16,8},{20,12},{25,17},{29,21},{17,9},{21,13},{26,... | collective-permute-start | bytes 1572872 | tf_op jit(solution)/shard_map/ppermute | solution.py:322
  594.3 15.3 %collective-permute-start.24 = (bf16[2,128,1024]{1,2,0:T(8,128)(2,1)}, bf16[2,128,1024]{1,2,0:T(8,128)(2,1)S(1)}, u32[]{:S(2)}, u32[]{:S(2)}) collective-permute-start(bf16[2,128,1024]{1,2,0:T(8,128)(2,1)} %fusion.50), channel_id=1, source_target_pairs={{0,8},{4,12},{8,16},{12,20},{16,24},{20,28},{1,9},{5,13},{9,17},{1... | collective-permute-start | bytes 1572872 | tf_op jit(solution)/shard_map/ppermute | solution.py:322
  600.7 15.0 %collective-permute-start.27 = (bf16[2,128,1024]{1,2,0:T(8,128)(2,1)}, bf16[2,128,1024]{1,2,0:T(8,128)(2,1)S(1)}, u32[]{:S(2)}, u32[]{:S(2)}) collective-permute-start(bf16[2,128,1024]{1,2,0:T(8,128)(2,1)} %fusion.48), channel_id=1, source_target_pairs={{24,16},{28,20},{16,8},{20,12},{8,0},{12,4},{25,17},{29,21},{17,9}... | collective-permute-start | bytes 1572872 | tf_op jit(solution)/shard_map/ppermute | solution.py:322
  605.9 14.2 %collective-permute-start.37 = (bf16[128,896]{1,0:T(8,128)(2,1)}, bf16[128,896]{1,0:T(8,128)(2,1)S(1)}, u32[]{:S(2)}, u32[]{:S(2)}) collective-permute-start(bf16[128,896]{1,0:T(8,128)(2,1)} %get-tuple-element.243), channel_id=1, source_target_pairs={{4,0},{12,8},{20,16},{28,24},{5,1},{13,9},{21,17},{29,25},{6,2},{1... | collective-permute-start | bytes 688136 | tf_op jit(solution)/shard_map/ppermute | solution.py:322
  618.2 8.3 %collective-permute-start.29 = (bf16[128,1024]{0,1:T(8,128)(2,1)S(1)}, bf16[128,1024]{0,1:T(8,128)(2,1)S(1)}, u32[]{:S(2)}, u32[]{:S(2)}) collective-permute-start(bf16[128,1024]{0,1:T(8,128)(2,1)S(1)} %get-tuple-element.237), channel_id=1, source_target_pairs={{4,0},{12,8},{20,16},{28,24},{5,1},{13,9},{21,17},{29,25},{6,2},{1... | collective-permute-start | bytes 786440 | tf_op jit(solution)/shard_map/ppermute | solution.py:322
  629.6 10.1 %collective-permute-start.50 = (bf16[2,128,896]{2,1,0:T(8,128)(2,1)S(1)}, bf16[2,128,896]{2,1,0:T(8,128)(2,1)S(1)}, u32[]{:S(2)}, u32[]{:S(2)}) collective-permute-start(bf16[2,128,896]{2,1,0:T(8,128)(2,1)S(1)} %get-tuple-element.196), channel_id=1, source_target_pairs={{0,8},{4,12},{1,9},{5,13},{2,10},{6,14},{3,11},{7,15}} | collective-permute-start | bytes 1376264 | tf_op jit(solution)/shard_map/ppermute | solution.py:322
  637.2 17.3 %collective-permute-start.38 = (bf16[2,320,1024]{2,1,0:T(8,128)(2,1)S(1)}, bf16[2,320,1024]{2,1,0:T(8,128)(2,1)S(1)}, u32[]{:S(2)}, u32[]{:S(2)}) collective-permute-start(bf16[2,320,1024]{2,1,0:T(8,128)(2,1)S(1)} %fusion.37), channel_id=1, source_target_pairs={{0,1},{1,0},{2,3},{3,2},{4,5},{5,4},{6,7},{7,6},{8,9},{9,8},{10,11... | collective-permute-start | bytes 3932168 | tf_op jit(solution)/shard_map/ppermute | solution.py:259
  639.6 23.0 %collective-permute-start.60 = (f32[128,256]{1,0:T(8,128)}, f32[128,256]{1,0:T(8,128)}, u32[]{:S(2)}, u32[]{:S(2)}) collective-permute-start(f32[128,256]{1,0:T(8,128)} %slice.443), channel_id=1, source_target_pairs={{0,1},{1,0},{2,3},{3,2},{4,5},{5,4},{6,7},{7,6},{8,9},{9,8},{10,11... | collective-permute-start | bytes 393224 | tf_op jit(solution)/shard_map/ppermute | solution.py:290
  639.8 11.9 %collective-permute-start.51 = (bf16[2,128,896]{2,1,0:T(8,128)(2,1)S(1)}, bf16[2,128,896]{2,1,0:T(8,128)(2,1)S(1)}, u32[]{:S(2)}, u32[]{:S(2)}) collective-permute-start(bf16[2,128,896]{2,1,0:T(8,128)(2,1)S(1)} %fusion.59), channel_id=1, source_target_pairs={{0,8},{4,12},{8,16},{12,20},{1,9},{5,13},{9,17},{13,21},{2,10},{6,... | collective-permute-start | bytes 1376264 | tf_op jit(solution)/shard_map/ppermute | solution.py:322
  652.9 15.9 %collective-permute-start.54 = (bf16[2,128,896]{2,1,0:T(8,128)(2,1)}, bf16[2,128,896]{2,1,0:T(8,128)(2,1)}, u32[]{:S(2)}, u32[]{:S(2)}) collective-permute-start(bf16[2,128,896]{2,1,0:T(8,128)(2,1)} %get-tuple-element.195), channel_id=1, source_target_pairs={{24,16},{28,20},{16,8},{20,12},{25,17},{29,21},{17,9},{21,13},{26,... | collective-permute-start | bytes 1376264 | tf_op jit(solution)/shard_map/ppermute | solution.py:322
  655.8 15.8 %collective-permute-start.39 = (bf16[320,1024]{1,0:T(8,128)(2,1)}, bf16[320,1024]{1,0:T(8,128)(2,1)}, u32[]{:S(2)}, u32[]{:S(2)}) collective-permute-start(bf16[320,1024]{1,0:T(8,128)(2,1)} %fusion.72), channel_id=1, source_target_pairs={{0,2},{1,3},{2,0},{3,1},{4,6},{5,7},{6,4},{7,5},{8,10},{9,11},{10,... | collective-permute-start | bytes 1966088 | tf_op jit(solution)/shard_map/ppermute | solution.py:259
  663.6 9.7 %collective-permute-start.61 = (f32[128,256]{1,0:T(8,128)S(1)}, f32[128,256]{1,0:T(8,128)S(1)}, u32[]{:S(2)}, u32[]{:S(2)}) collective-permute-start(f32[128,256]{1,0:T(8,128)S(1)} %slice_add_fusion.3), channel_id=1, source_target_pairs={{0,2},{1,3},{2,0},{3,1},{4,6},{5,7},{6,4},{7,5},{8,10},{9,11},{10,... | collective-permute-start | bytes 393224 | tf_op jit(solution)/shard_map/ppermute | solution.py:290
  664.5 15.6 %collective-permute-start.52 = (bf16[2,128,896]{2,1,0:T(8,128)(2,1)}, bf16[2,128,896]{2,1,0:T(8,128)(2,1)S(1)}, u32[]{:S(2)}, u32[]{:S(2)}) collective-permute-start(bf16[2,128,896]{2,1,0:T(8,128)(2,1)} %get-tuple-element.194), channel_id=1, source_target_pairs={{0,8},{4,12},{8,16},{12,20},{16,24},{20,28},{1,9},{5,13},{9,17},{1... | collective-permute-start | bytes 1376264 | tf_op jit(solution)/shard_map/ppermute | solution.py:322
  670.2 11.6 %collective-permute-start.55 = (bf16[2,128,896]{2,1,0:T(8,128)(2,1)S(1)}, bf16[2,128,896]{2,1,0:T(8,128)(2,1)S(1)}, u32[]{:S(2)}, u32[]{:S(2)}) collective-permute-start(bf16[2,128,896]{2,1,0:T(8,128)(2,1)S(1)} %fusion.58), channel_id=1, source_target_pairs={{24,16},{28,20},{16,8},{20,12},{8,0},{12,4},{25,17},{29,21},{17,9}... | collective-permute-start | bytes 1376264 | tf_op jit(solution)/shard_map/ppermute | solution.py:322
  685.2 9.0 %collective-permute-start.56 = (bf16[128,896]{1,0:T(8,128)(2,1)S(1)}, bf16[128,896]{1,0:T(8,128)(2,1)S(1)}, u32[]{:S(2)}, u32[]{:S(2)}) collective-permute-start(bf16[128,896]{1,0:T(8,128)(2,1)S(1)} %get-tuple-element.240), channel_id=1, source_target_pairs={{0,4},{8,12},{16,20},{24,28},{1,5},{9,13},{17,21},{25,29},{2,6},{1... | collective-permute-start | bytes 688136 | tf_op jit(solution)/shard_map/ppermute | solution.py:322
  (195 other events, 2148.1 us)
Sparse Core Ops, SparseCore 0:
  11.7 60.3 all-gather.4
  74.7 38.1 all-gather.6
  119.4 56.5 all-gather.8
  178.5 38.1 all-gather.10
